TPU v7x, 1024 devices: a whole 4x8x16 slice. The times are simulated.
1024 devices in a mesh: grp: 16 (over z), sub: 64 (over y, x, core).
Axes of the slice: x: 4, y: 8, z: 16, core: 2. Of those that a mesh axis runs over, the one named last changes fastest.
Arguments:
- basis: bfloat16 [16, 64, 48, 8192], P('grp', 'sub'), may hold values from -1.1953125 to 1.1953125
- bdiag: float32 [16, 64, 8192], P('grp', 'sub'), may hold values from 1 to 4
- interior: bfloat16 [64, 8192, 512], P('sub'), may hold values from -0.125 to 0.125
- send_tiles: int32 [16, 64, 64, 1], P('grp', 'sub'), may hold values from 0 to 63
- land_tiles: int32 [16, 64, 64, 1], P('grp', 'sub'), may hold values from 0 to 63
- send_counts: int32 [16, 64, 64], P('grp', 'sub'), may hold values from 0 to 1, as said below
- mortar_weight: bfloat16 [16, 64, 64, 1, 128], P('grp', 'sub'), may hold values from 0.099609375 to 1.8984375
- face_tiles: int32 [16, 64, 2, 4], P('grp', 'sub'), may hold values from 0 to 63
- owner_map: int32 [16], P('grp'), may hold values from 0 to 15
Outputs:
- coupling_in: bfloat16 [16, 64, 64, 2304], P('grp', 'sub')
- coupling_out: bfloat16 [16, 64, 64, 2304], P('grp', 'sub')
- owned: float32 [16, 64, 2304], P('grp', 'sub')
Inputs may be any that keep to these rules, and one draw needn't show every extreme that they name: send_counts[g, s, s] = 0; a pair's count can reach 1.
All inputs are finite; a program needn't handle non-finite values.
Results may differ from a plain program's by a relative error of at most 0.01.
Values may be sent and summed in bfloat16 or wider, within the bound.
No kernel may reach another device: no remote copies, remote signals or barrier semaphores. Data moves between devices by JAX's collectives and lax.ppermute only.
A program may use at most 32 MiB of HBM per device.

v0:
```python
import jax
import jax.numpy as jnp
from jax import lax
from jax.sharding import PartitionSpec as P


def shifted(value, axis, steps):
    count = lax.axis_size(axis)
    leading, last = (max(0, -steps), min(count, count - steps))
    return lax.ppermute(value, axis, [(source, source + steps) for source in range(leading, last)])


def per_device(
    basis,
    bdiag,
    interior,
    send_tiles,
    land_tiles,
    send_counts,
    mortar_weight,
    face_tiles,
    owner_map,
):
    basis_rows = basis[0, 0]
    factor = interior[0]
    vectors = basis_rows.shape[0]
    interface = basis_rows.shape[1]
    tile_count = interface // 128
    reduced = jnp.dot(basis_rows, factor, preferred_element_type=jnp.float32).astype(jnp.bfloat16)
    correction = lax.dot_general(
        reduced, factor, (((1,), (1,)), ((), ())), preferred_element_type=jnp.float32
    )
    schur_rows = (basis_rows.astype(jnp.float32) * bdiag[0, 0][None, :] - correction).astype(
        jnp.bfloat16
    )
    zpanel = schur_rows.reshape(vectors, tile_count, 128).transpose(1, 0, 2)
    bpanel = basis_rows.reshape(vectors, tile_count, 128).transpose(1, 0, 2)
    shared = send_counts[0, 0]
    capacity = send_tiles.shape[3]
    partners = send_tiles.shape[2]
    active = (jnp.arange(capacity)[None, :] < shared[:, None]).astype(jnp.float32)
    picked = zpanel[send_tiles[0, 0]]
    weighted = (
        picked.astype(jnp.float32)
        * mortar_weight[0, 0].astype(jnp.float32)[:, :, None, :]
        * active[:, :, None, None]
    ).astype(jnp.bfloat16)
    arrived, landing = (
        lax.all_to_all(weighted, "sub", split_axis=0, concat_axis=0, tiled=True),
        lax.all_to_all(land_tiles[0, 0], "sub", split_axis=0, concat_axis=0, tiled=True),
    )
    own_tiles = bpanel[landing]
    blocks = jnp.einsum("scki,scli->skl", arrived, own_tiles, preferred_element_type=jnp.float32)
    coupling_in = blocks.astype(jnp.bfloat16).reshape(partners, vectors * vectors)
    coupling_out = lax.all_to_all(coupling_in, "sub", split_axis=0, concat_axis=0, tiled=True)
    outgoing = zpanel[face_tiles[0, 0, 1]]
    incoming = shifted(outgoing, "grp", 1)
    face_block = jnp.einsum(
        "jki,jli->kl", incoming, bpanel[face_tiles[0, 0, 0]], preferred_element_type=jnp.float32
    ).reshape(vectors * vectors)
    chosen = (jnp.arange(lax.axis_size("grp")) == owner_map[0]).astype(jnp.float32)
    owned = lax.psum_scatter(
        (chosen[:, None] * face_block[None, :]).astype(jnp.bfloat16),
        "grp",
        scatter_dimension=0,
        tiled=True,
    ).astype(jnp.float32)
    owned = owned[None]
    return (coupling_in[None, None], coupling_out[None, None], owned)


def solution(mesh):
    placed = (
        P("grp", "sub", None, None),
        P("grp", "sub", None),
        P("sub", None, None),
        P("grp", "sub", None, None),
        P("grp", "sub", None, None),
        P("grp", "sub", None),
        P("grp", "sub", None, None, None),
        P("grp", "sub", None, None),
        P("grp"),
    )
    return jax.shard_map(
        per_device,
        mesh=mesh,
        in_specs=placed,
        out_specs=(P("grp", "sub", None, None), P("grp", "sub", None, None), P("grp", "sub", None)),
        check_vma=False,
    )
```

profile of v0, /device:TPU:2, one launch (start us, length us, event | category | flops | bytes accessed | tf_op | source)
XLA Modules:
  0.0 239.3 jit_solution(697891936232073270)
XLA Ops:
  7.2 1.4 copy.26
  8.5 17.2 %all-to-all-start.1 = ((s32[64,1,1]{2,1,0:T(1,128)}), s32[64,1,1]{2,1,0:T(1,128)S(1)}, u32[]{:S(2)}, u32[]{:S(2)}) async-start(s32[64,1,1]{2,1,0:T(1,128)} %copy.26), calls=%async_computation.1 | async-start | bytes 65536 | tf_op jit(solution)/shard_map/all_to_all | solution.py:50
  25.7 10.2 %fusion.6 = bf16[6,64,8,128]{3,2,1,0:T(8,128)(2,1)S(1)} fusion(bf16[1,8192,512]{2,1,0:T(8,128)(2,1)} %param.11, bf16[1,1,48,8192]{3,2,1,0:T(8,128)(2,1)} %param.9, f32[8192]{0:T(1024)} %bitcast.80), kind=kOutput, calls=%fused_computation.13 | convolution fusion | flops 806903808 | bytes 9994240 | tf_op jit(solution)/shard_map/dot_general | solution.py:30
  36.0 0.1 copy.37
  36.2 0.5 copy-done.3
  36.7 0.1 copy-done.1
  36.7 0.7 gather_fusion
  37.5 1.1 fusion.14
  38.6 10.4 %all-to-all-start = ((bf16[64,1,48,128]{3,2,1,0:T(8,128)(2,1)}), bf16[64,1,48,128]{3,2,1,0:T(8,128)(2,1)S(1)}, u32[]{:S(2)}, u32[]{:S(2)}) async-start(bf16[64,1,48,128]{3,2,1,0:T(8,128)(2,1)} %fusion.14), calls=%async_computation | async-start | bytes 1572864 | tf_op jit(solution)/shard_map/all_to_all | solution.py:49
  49.0 0.6 gather_fusion.2
  49.6 1.3 collective-permute-start
  50.9 0.2 copy.33
  51.1 0.5 copy.38
  52.3 0.6 gather_fusion.3
  52.9 0.1 copy.27
  53.0 0.7 gather_fusion.1
  53.7 0.1 convolution_bitcast_fusion
  53.8 0.1 mul.65
  53.9 18.3 %all-to-all-done = bf16[64,1,48,128]{3,2,1,0:T(8,128)(2,1)S(1)} async-done(((bf16[64,1,48,128]{3,2,1,0:T(8,128)(2,1)}), bf16[64,1,48,128]{3,2,1,0:T(8,128)(2,1)S(1)}, u32[]{:S(2)}, u32[]{:S(2)}) %all-to-all-start) | async-done | bytes 786464 | tf_op jit(solution)/shard_map/all_to_all | solution.py:49
  72.2 0.5 convolution_convert_fusion
  72.7 1.0 all_to_all.20
  73.8 0.5 broadcast.126
  74.3 2.4 reduce
  76.7 0.8 reshape.224
  77.5 5.8 %all-to-all-start.2 = ((bf16[64,2,1152]{2,1,0:T(2,128)(2,1)}), bf16[64,2,1152]{2,1,0:T(2,128)(2,1)S(1)}, u32[]{:S(2)}, u32[]{:S(2)}) async-start(bf16[64,2,1152]{2,1,0:T(2,128)(2,1)} %reshape.224), calls=%async_computation.2 | async-start | bytes 589824 | tf_op jit(solution)/shard_map/all_to_all | solution.py:55
  83.3 0.7 multiply_convert_fusion
  84.1 1.3 dynamic-slice
  85.4 142.6 %all-reduce.3.cloned.1.call-done = bf16[16,2304]{1,0:T(8,128)(2,1)} async-done(((bf16[16,2304]{1,0:T(8,128)(2,1)}), bf16[16,2304]{1,0:T(8,128)(2,1)}) %all-reduce.3.cloned.1.call-update) | async-done | bytes 73744
  228.0 2.0 bitcast_convert_fusion.1
  230.0 1.5 broadcast_in_dim_reshape.4
  231.5 0.2 reshape.225
  231.7 0.7 copy.39
  (23 shorter events, 0.1 us)
Async XLA Ops:
  8.5 30.1 %all-to-all-start.1 = ((s32[64,1,1]{2,1,0:T(1,128)}), s32[64,1,1]{2,1,0:T(1,128)S(1)}, u32[]{:S(2)}, u32[]{:S(2)}) async-start(s32[64,1,1]{2,1,0:T(1,128)} %copy.26), calls=%async_computation.1 | async-start | bytes 65536 | tf_op jit(solution)/shard_map/all_to_all | solution.py:50
  36.0 0.7 copy-start.3
  36.0 0.7 copy-start.1
  36.0 0.7 copy-start.4
  37.4 11.6 %copy-start.2 = (s32[1,1,2,4]{3,2,1,0:T(2,128)S(1)}, s32[1,1,2,4]{3,2,1,0:T(2,128)}, u32[]{:S(2)}) copy-start(s32[1,1,2,4]{3,2,1,0:T(2,128)} %param.16) | copy-start | bytes 100
  37.4 13.5 %copy-start = (bf16[1,1,48,8192]{3,2,1,0:T(8,128)(2,1)S(1)}, bf16[1,1,48,8192]{3,2,1,0:T(8,128)(2,1)}, u32[]{:S(2)}) copy-start(bf16[1,1,48,8192]{3,2,1,0:T(8,128)(2,1)} %param.9) | copy-start | bytes 2359300
  38.6 33.6 %all-to-all-start = ((bf16[64,1,48,128]{3,2,1,0:T(8,128)(2,1)}), bf16[64,1,48,128]{3,2,1,0:T(8,128)(2,1)S(1)}, u32[]{:S(2)}, u32[]{:S(2)}) async-start(bf16[64,1,48,128]{3,2,1,0:T(8,128)(2,1)} %fusion.14), calls=%async_computation | async-start | bytes 1572864 | tf_op jit(solution)/shard_map/all_to_all | solution.py:49
  49.6 4.1 %collective-permute-start = (bf16[4,48,128]{2,1,0:T(8,128)(2,1)S(1)}, bf16[4,48,128]{2,1,0:T(8,128)(2,1)S(1)}, u32[]{:S(2)}, u32[]{:S(2)}) collective-permute-start(bf16[4,48,128]{2,1,0:T(8,128)(2,1)S(1)} %gather_fusion.2), channel_id=1, source_target_pairs={{0,64},{64,128},{128,192},{192,256},{256,320},{320,384},{384,448},... | collective-permute-start | bytes 147464 | tf_op jit(solution)/shard_map/ppermute | solution.py:10
  77.5 154.0 %all-to-all-start.2 = ((bf16[64,2,1152]{2,1,0:T(2,128)(2,1)}), bf16[64,2,1152]{2,1,0:T(2,128)(2,1)S(1)}, u32[]{:S(2)}, u32[]{:S(2)}) async-start(bf16[64,2,1152]{2,1,0:T(2,128)(2,1)} %reshape.224), calls=%async_computation.2 | async-start | bytes 589824 | tf_op jit(solution)/shard_map/all_to_all | solution.py:55
  83.3 144.7 %all-reduce.3.cloned.1.call-start = ((), (), s32[]{:S(2)}) async-start(), calls=%async_computation.3 | async-start | bytes 147456
Sparse Core Ops, SparseCore 0:
  87.0 140.9 all-reduce.2
where the time goes:
time: 240 us; the launch traced here: 239 us
  waiting for transfers between devices  161 us (67%)
  starting transfers between devices  34.8 us (14%)
  between operations  14.9 us (6%)
  local copies, waits for them, and re-layouts  11.6 us (5%)
  matrix products  10.9 us (5%)
  other arithmetic  6.28 us (3%)
    unnamed x2, waiting for transfers between devices  143 us
    all_to_all x1, waiting for transfers between devices, per_device(): lax.all_to_all(weighted, 'sub', split_axis=0, concat_axis=0, tiled=True)  18.3 us
    all_to_all x1, starting transfers between devices, per_device(): lax.all_to_all(land_tiles[0, 0], 'sub', split_axis=0, concat_axis=0, tile...  17.2 us
    all_to_all x1, starting transfers between devices, per_device(): lax.all_to_all(weighted, 'sub', split_axis=0, concat_axis=0, tiled=True)  10.4 us
    dot_general x1, matrix products, per_device(): lax.dot_general(reduced, factor, (((1,), (1,)), ((), ())), preferred_elem...  10.2 us
    all_to_all x1, starting transfers between devices, per_device(): lax.all_to_all(coupling_in, 'sub', split_axis=0, concat_axis=0, tiled=True)  5.82 us
  transfers between devices with their start and end apart: 5, of which 2 were waited for; matrix products, arithmetic and copies ran while one was open for 9% of the time, Pallas kernels for 0%

commit v1 on v0

v1 whole, which is shorter than its diff:
```python
import jax
import jax.numpy as jnp
from jax import lax
from jax.experimental import pallas as pl
from jax.experimental.pallas import tpu as pltpu
from jax.sharding import PartitionSpec as P

LANES = 128
INDEX_ROWS = 8
CHUNKS = 8
HALF_LANES = 64


def dot_nt(a, b):
    return lax.dot_general(a, b, (((1,), (1,)), ((), ())), preferred_element_type=jnp.float32)


def schur_kernel(
    basis_hbm, bdiag_hbm, interior_hbm, weight_hbm, send_hbm, count_hbm, land_hbm, face_hbm,
    payload_ref, faces_ref,
    basis_ref, bdiag_ref, interior_ref, weight_ref, send_ref, count_ref, land_ref, face_ref,
    tiles_ref, scaled_ref, sems, small_sems,
):
    vectors, interface = basis_ref.shape
    partners = payload_ref.shape[0]
    chunk = interface // CHUNKS
    basis_copy = pltpu.make_async_copy(basis_hbm, basis_ref, sems.at[CHUNKS])
    basis_copy.start()
    chunk_copies = []
    for i in range(CHUNKS):
        rows = pl.ds(i * chunk, chunk)
        chunk_copies.append(pltpu.make_async_copy(interior_hbm.at[rows], interior_ref.at[rows], sems.at[i]))
        chunk_copies[-1].start()
    small = [
        (bdiag_hbm, bdiag_ref), (weight_hbm, weight_ref), (send_hbm, send_ref),
        (count_hbm, count_ref), (land_hbm, land_ref), (face_hbm, face_ref),
    ]
    small_copies = [pltpu.make_async_copy(a, b, small_sems.at[i]) for i, (a, b) in enumerate(small)]
    for copy in small_copies:
        copy.start()
    basis_copy.wait()
    total = jnp.zeros((vectors, interior_ref.shape[1]), jnp.float32)
    for i in range(CHUNKS):
        chunk_copies[i].wait()
        total += jnp.dot(
            basis_ref[:, i * chunk : (i + 1) * chunk],
            interior_ref[i * chunk : (i + 1) * chunk, :],
            preferred_element_type=jnp.float32,
        )
    reduced = total.astype(jnp.bfloat16)
    for copy in small_copies:
        copy.wait()
    for i in range(CHUNKS):
        cols = slice(i * chunk, (i + 1) * chunk)
        correction = dot_nt(reduced, interior_ref[cols, :])
        schur = (basis_ref[:, cols].astype(jnp.float32) * bdiag_ref[:, cols] - correction).astype(jnp.bfloat16)
        for j in range(chunk // LANES):
            tiles_ref[i * (chunk // LANES) + j] = schur[:, j * LANES : (j + 1) * LANES]
    scaled_ref[...] = weight_ref[...].astype(jnp.float32)

    def one(p, carry):
        active = (count_ref[0, p] > 0).astype(jnp.float32)
        row = scaled_ref[pl.ds(p, 1), :] * active
        tile = tiles_ref[send_ref[0, p]].astype(jnp.float32)
        payload_ref[p, 0:vectors, :] = (tile * row).astype(jnp.bfloat16)
        landing = land_ref[0, p].astype(jnp.float32)
        payload_ref[p, vectors : vectors + INDEX_ROWS, :] = jnp.full(
            (INDEX_ROWS, LANES), landing, jnp.float32
        ).astype(jnp.bfloat16)
        return carry

    lax.fori_loop(0, partners, one, 0, unroll=4)
    for j in range(faces_ref.shape[0]):
        faces_ref[j] = tiles_ref[face_ref[1, j]]


def schur_tiles(basis, bdiag, interior, weights, send, counts, land, face):
    vectors, interface = basis.shape
    partners = weights.shape[0]
    operands = (basis, bdiag, interior, weights, send, counts, land, face)
    return pl.pallas_call(
        schur_kernel,
        out_shape=(
            jax.ShapeDtypeStruct((partners, vectors + INDEX_ROWS, LANES), jnp.bfloat16),
            jax.ShapeDtypeStruct((face.shape[1], vectors, LANES), jnp.bfloat16),
        ),
        in_specs=[pl.BlockSpec(memory_space=pltpu.HBM)] * len(operands),
        out_specs=[pl.BlockSpec(memory_space=pltpu.VMEM)] * 2,
        scratch_shapes=[
            pltpu.VMEM(basis.shape, basis.dtype),
            pltpu.VMEM(bdiag.shape, bdiag.dtype),
            pltpu.VMEM(interior.shape, interior.dtype),
            pltpu.VMEM(weights.shape, weights.dtype),
            pltpu.SMEM(send.shape, jnp.int32),
            pltpu.SMEM(counts.shape, jnp.int32),
            pltpu.SMEM(land.shape, jnp.int32),
            pltpu.SMEM(face.shape, jnp.int32),
            pltpu.VMEM((interface // LANES, vectors, LANES), jnp.bfloat16),
            pltpu.VMEM(weights.shape, jnp.float32),
            pltpu.SemaphoreType.DMA((CHUNKS + 1,)),
            pltpu.SemaphoreType.DMA((6,)),
        ],
        compiler_params=pltpu.CompilerParams(vmem_limit_bytes=60 * 1024 * 1024),
        name="schur_tiles",
    )(*operands)


def block_kernel(arrived_ref, basis_ref, packed_ref, index_ref, landing_ref, sem):
    vectors = basis_ref.shape[0]
    partners = arrived_ref.shape[0]
    half = vectors // 2
    marks = arrived_ref[:, vectors : vectors + INDEX_ROWS, :].astype(jnp.float32)
    index_ref[...] = jnp.max(marks, axis=1).astype(jnp.int32)
    copy = pltpu.make_async_copy(index_ref, landing_ref, sem)
    copy.start()
    copy.wait()
    gap = jnp.zeros((HALF_LANES - vectors, LANES), jnp.bfloat16)
    left = lax.broadcasted_iota(jnp.int32, (half, LANES), 1) < HALF_LANES

    def one(s, carry):
        start = pl.multiple_of(landing_ref[s, 0] * LANES, LANES)
        tile = basis_ref[:, pl.ds(start, LANES)]
        twice = jnp.concatenate([tile, gap, tile, gap], axis=0)
        block = dot_nt(arrived_ref[s, 0:vectors, :], twice)
        packed_ref[s] = jnp.where(left, block[:half], block[half:]).astype(jnp.bfloat16)
        return carry

    lax.fori_loop(0, partners, one, 0, unroll=8)


def coupling_blocks(arrived, basis):
    partners = arrived.shape[0]
    return pl.pallas_call(
        block_kernel,
        out_shape=jax.ShapeDtypeStruct((partners, basis.shape[0] // 2, LANES), jnp.bfloat16),
        in_specs=[pl.BlockSpec(memory_space=pltpu.VMEM)] * 2,
        out_specs=pl.BlockSpec(memory_space=pltpu.VMEM),
        scratch_shapes=[
            pltpu.VMEM((partners, LANES), jnp.int32),
            pltpu.SMEM((partners, LANES), jnp.int32),
            pltpu.SemaphoreType.DMA,
        ],
        compiler_params=pltpu.CompilerParams(vmem_limit_bytes=32 * 1024 * 1024),
        name="coupling_blocks",
    )(arrived, basis)


def unpack(packed, vectors):
    both = jnp.concatenate(
        [packed[..., :vectors], packed[..., HALF_LANES : HALF_LANES + vectors]], axis=-2
    )
    return both.reshape(both.shape[:-2] + (vectors * vectors,))


def per_device(
    basis,
    bdiag,
    interior,
    send_tiles,
    land_tiles,
    send_counts,
    mortar_weight,
    face_tiles,
    owner_map,
):
    basis_rows = basis[0, 0]
    vectors, interface = basis_rows.shape
    partners = send_tiles.shape[2]
    groups = lax.axis_size("grp")
    payload, outgoing = schur_tiles(
        basis_rows,
        bdiag.reshape(1, interface),
        interior[0],
        mortar_weight.reshape(partners, LANES),
        send_tiles.reshape(1, partners),
        send_counts.reshape(1, partners),
        land_tiles.reshape(1, partners),
        face_tiles[0, 0],
    )
    arrived = lax.all_to_all(payload, "sub", split_axis=0, concat_axis=0, tiled=True)

    incoming = lax.ppermute(outgoing, "grp", [(g, g + 1) for g in range(groups - 1)])
    own = jnp.stack(
        [
            lax.dynamic_slice(basis_rows, (0, face_tiles[0, 0, 0, j] * LANES), (vectors, LANES))
            for j in range(face_tiles.shape[3])
        ]
    )
    face = jnp.einsum("jki,jli->kl", incoming, own, preferred_element_type=jnp.float32)
    half = vectors // 2
    pad = jnp.zeros((half, HALF_LANES - vectors), jnp.bfloat16)
    small = face.astype(jnp.bfloat16)
    small = jnp.concatenate([small[:half], pad, small[half:], pad], axis=1)
    owner = jnp.full((INDEX_ROWS, LANES), owner_map[0], jnp.int32).astype(jnp.bfloat16)
    gathered = jnp.concatenate([small, owner], axis=0)[None]
    step = groups // 2
    while step >= 1:
        other = lax.ppermute(gathered, "grp", [(g, (g + step) % groups) for g in range(groups)])
        gathered = jnp.concatenate([gathered, other], axis=0)
        step //= 2
    mine = gathered[:, half, 0] == lax.axis_index("grp").astype(jnp.bfloat16)
    owned = jnp.sum(
        jnp.where(mine[:, None, None], gathered[:, :half].astype(jnp.float32), 0.0), axis=0
    )
    owned = unpack(owned, vectors)[None, None]

    packed = coupling_blocks(arrived, basis_rows)
    returned = lax.all_to_all(packed, "sub", split_axis=0, concat_axis=0, tiled=True)
    coupling_in = unpack(packed, vectors)
    coupling_out = unpack(returned, vectors)
    return (coupling_in[None, None], coupling_out[None, None], owned)


def solution(mesh):
    placed = (
        P("grp", "sub", None, None),
        P("grp", "sub", None),
        P("sub", None, None),
        P("grp", "sub", None, None),
        P("grp", "sub", None, None),
        P("grp", "sub", None),
        P("grp", "sub", None, None, None),
        P("grp", "sub", None, None),
        P("grp"),
    )
    return jax.shard_map(
        per_device,
        mesh=mesh,
        in_specs=placed,
        out_specs=(P("grp", "sub", None, None), P("grp", "sub", None, None), P("grp", "sub", None)),
        check_vma=False,
    )
```

time: 240 us -> 112 us (0.47)
  the two profiles are of different devices: /device:TPU:2 before, /device:TPU:1 now
where the time goes in v1:
time: 112 us; the launch traced here: 111 us
  starting transfers between devices  60.5 us (54%)
  waiting for transfers between devices  27.7 us (25%)
  Pallas kernels  12.1 us (11%)
  local copies, waits for them, and re-layouts  5.88 us (5%)
  between operations  4.12 us (4%)
    ppermute x4, starting transfers between devices, per_device(): lax.ppermute(gathered, 'grp', [(g, (g + step) % groups) for g in range(gr...  26.3 us
    all_to_all x1, starting transfers between devices, per_device(): lax.all_to_all(payload, 'sub', split_axis=0, concat_axis=0, tiled=True)  18.4 us
    ppermute x4, waiting for transfers between devices, per_device(): lax.ppermute(gathered, 'grp', [(g, (g + step) % groups) for g in range(gr...  16.4 us
    all_to_all x1, starting transfers between devices, per_device(): lax.all_to_all(packed, 'sub', split_axis=0, concat_axis=0, tiled=True)  14.6 us
    all_to_all x1, waiting for transfers between devices, per_device(): lax.all_to_all(packed, 'sub', split_axis=0, concat_axis=0, tiled=True)  11.3 us
    pallas_call x1, Pallas kernels, schur_tiles(): pl.pallas_call(schur_kernel, out_shape=(jax.ShapeDtypeStruct((partners, v...  7.96 us
    pallas_call x1, Pallas kernels, coupling_blocks(): pl.pallas_call(block_kernel, out_shape=jax.ShapeDtypeStruct((partners, ba...  4.15 us
    another operation x2, local copies, waits for them, and re-layouts, per_device(): return (coupling_in[None, None], coupling_out[None, None], owned)  2.96 us
  transfers between devices with their start and end apart: 7, of which 5 were waited for; matrix products, arithmetic and copies ran while one was open for 5% of the time, Pallas kernels for 0%

profile of v1, /device:TPU:1, one launch (start us, length us, event | category | flops | bytes accessed | tf_op | source)
XLA Modules:
  0.0 111.3 jit_solution(14908447060568322544)
XLA Ops:
  0.6 8.0 %schur_tiles.1 = (bf16[64,56,128]{2,1,0:T(8,128)(2,1)}, bf16[4,48,128]{2,1,0:T(8,128)(2,1)}) custom-call(bf16[48,8192]{1,0:T(8,128)(2,1)} %bitcast.29, f32[1,8192]{1,0:T(1,128)} %bitcast.32, bf16[8192,512]{1,0:T(8,128)(2,1)} %bitcast.31, bf16[64,128]{1,0:T(8,128)(2,1)} %bitcast.33, s32[1,64]{1,0:T(1,128)} %bitcast.35, s32[1,64]{1,0:T(1,128)} %bitcast.36, ...), custom_call_target="tpu_custom_call" | custom-call | tf_op jit(solution)/shard_map/schur_tiles/pallas_call | solution.py:81
  8.6 0.0 copy-start.2
  8.6 0.0 copy-start.1
  8.6 0.0 copy-start
  8.6 18.4 %all-to-all-start = ((bf16[64,56,128]{2,1,0:T(8,128)(2,1)}), bf16[64,56,128]{2,1,0:T(8,128)(2,1)S(1)}, u32[]{:S(2)}, u32[]{:S(2)}) async-start(bf16[64,56,128]{2,1,0:T(8,128)(2,1)} %get-tuple-element.5), calls=%async_computation | async-start | bytes 1835008 | tf_op jit(solution)/shard_map/all_to_all | solution.py:180
  27.0 1.3 %collective-permute-start = (bf16[4,48,128]{2,1,0:T(8,128)(2,1)S(1)}, bf16[4,48,128]{2,1,0:T(8,128)(2,1)S(1)}, u32[]{:S(2)}, u32[]{:S(2)}) collective-permute-start(bf16[4,48,128]{2,1,0:T(8,128)(2,1)S(1)} %copy-done.2), channel_id=1, source_target_pairs={{0,64},{64,128},{128,192},{192,256},{256,320},{320,384},{384,448},... | collective-permute-start | bytes 147464 | tf_op jit(solution)/shard_map/ppermute | solution.py:182
  28.3 0.6 fusion.22
  32.2 0.0 collective-permute-done
  32.3 0.1 fusion
  32.4 0.1 constant_dynamic-update-slice_fusion.4
  32.5 14.3 %collective-permute-start.1 = (bf16[1,32,128]{2,1,0:T(8,128)(2,1)S(1)}, bf16[1,32,128]{2,1,0:T(8,128)(2,1)S(1)}, u32[]{:S(2)}, u32[]{:S(2)}) collective-permute-start(bf16[1,32,128]{2,1,0:T(8,128)(2,1)S(1)} %get-tuple-element.8), channel_id=1, source_target_pairs={{0,512},{64,576},{128,640},{192,704},{256,768},{320,832},{384,896}... | collective-permute-start | bytes 24584 | tf_op jit(solution)/shard_map/ppermute | solution.py:198
  46.8 1.0 collective-permute-done.1
  47.8 5.8 %collective-permute-start.2 = (bf16[2,32,128]{2,1,0:T(8,128)(2,1)S(1)}, bf16[2,32,128]{2,1,0:T(8,128)(2,1)S(1)}, u32[]{:S(2)}, u32[]{:S(2)}) collective-permute-start(bf16[2,32,128]{2,1,0:T(8,128)(2,1)S(1)} %pad_maximum_fusion.5), channel_id=1, source_target_pairs={{0,256},{64,320},{128,384},{192,448},{256,512},{320,576},{384,640}... | collective-permute-start | bytes 49160 | tf_op jit(solution)/shard_map/ppermute | solution.py:198
  53.6 6.2 %collective-permute-done.2 = bf16[2,32,128]{2,1,0:T(8,128)(2,1)S(1)} collective-permute-done((bf16[2,32,128]{2,1,0:T(8,128)(2,1)S(1)}, bf16[2,32,128]{2,1,0:T(8,128)(2,1)S(1)}, u32[]{:S(2)}, u32[]{:S(2)}) %collective-permute-start.2) | collective-permute-done | bytes 16416 | tf_op jit(solution)/shard_map/ppermute | solution.py:198
  59.9 4.3 %collective-permute-start.3 = (bf16[4,32,128]{2,1,0:T(8,128)(2,1)S(1)}, bf16[4,32,128]{2,1,0:T(8,128)(2,1)S(1)}, u32[]{:S(2)}, u32[]{:S(2)}) collective-permute-start(bf16[4,32,128]{2,1,0:T(8,128)(2,1)S(1)} %pad_maximum_fusion.3), channel_id=1, source_target_pairs={{0,128},{64,192},{128,256},{192,320},{256,384},{320,448},{384,512}... | collective-permute-start | bytes 98312 | tf_op jit(solution)/shard_map/ppermute | solution.py:198
  64.2 4.9 %collective-permute-done.3 = bf16[4,32,128]{2,1,0:T(8,128)(2,1)S(1)} collective-permute-done((bf16[4,32,128]{2,1,0:T(8,128)(2,1)S(1)}, bf16[4,32,128]{2,1,0:T(8,128)(2,1)S(1)}, u32[]{:S(2)}, u32[]{:S(2)}) %collective-permute-start.3) | collective-permute-done | bytes 32800 | tf_op jit(solution)/shard_map/ppermute | solution.py:198
  69.1 1.9 %collective-permute-start.4 = (bf16[8,32,128]{2,1,0:T(8,128)(2,1)S(1)}, bf16[8,32,128]{2,1,0:T(8,128)(2,1)S(1)}, u32[]{:S(2)}, u32[]{:S(2)}) collective-permute-start(bf16[8,32,128]{2,1,0:T(8,128)(2,1)S(1)} %pad_maximum_fusion.2), channel_id=1, source_target_pairs={{0,64},{64,128},{128,192},{192,256},{256,320},{320,384},{384,448},... | collective-permute-start | bytes 196616 | tf_op jit(solution)/shard_map/ppermute | solution.py:198
  71.0 4.3 %collective-permute-done.4 = bf16[8,32,128]{2,1,0:T(8,128)(2,1)S(1)} collective-permute-done((bf16[8,32,128]{2,1,0:T(8,128)(2,1)S(1)}, bf16[8,32,128]{2,1,0:T(8,128)(2,1)S(1)}, u32[]{:S(2)}, u32[]{:S(2)}) %collective-permute-start.4) | collective-permute-done | bytes 65568 | tf_op jit(solution)/shard_map/ppermute | solution.py:198
  75.3 0.4 compare_reduce_fusion
  75.7 0.0 all-to-all-done.arrived_ref
  75.7 4.2 %coupling_blocks.1 = bf16[64,24,128]{2,1,0:T(8,128)(2,1)} custom-call(bf16[64,56,128]{2,1,0:T(8,128)(2,1)S(1)} %all-to-all-done.arrived_ref, bf16[48,8192]{1,0:T(8,128)(2,1)S(1)} %bitcast.30), custom_call_target="tpu_custom_call" | custom-call | tf_op jit(solution)/shard_map/coupling_blocks/pallas_call | solution.py:133
  79.9 14.6 %all-to-all-start.1 = ((bf16[64,24,128]{2,1,0:T(8,128)(2,1)}), bf16[64,24,128]{2,1,0:T(8,128)(2,1)S(1)}, u32[]{:S(2)}, u32[]{:S(2)}) async-start(bf16[64,24,128]{2,1,0:T(8,128)(2,1)} %coupling_blocks.1), calls=%async_computation.1 | async-start | bytes 786432 | tf_op jit(solution)/shard_map/all_to_all | solution.py:208
  94.5 0.1 select_reduce_fusion
  94.6 0.1 fusion.20
  94.6 0.7 broadcast_in_dim_reshape.11
  95.3 1.3 %fusion.19 = (bf16[64,24,48]{2,1,0:T(8,128)(2,1)S(1)}, bf16[64,24,48]{2,1,0:T(8,128)(2,1)S(1)}) fusion(bf16[64,24,128]{2,1,0:T(8,128)(2,1)} %coupling_blocks.1), kind=kLoop, calls=%fused_computation.37 | loop fusion | bytes 589824 | tf_op jit(solution)/shard_map/slice | solution.py:150
  96.6 0.2 pad_maximum_fusion
  96.8 1.5 %broadcast_in_dim_reshape.9 = bf16[1,1,64,2304]{3,2,1,0:T(8,128)(2,1)} reshape(bf16[64,48,48]{2,1,0:T(8,128)(2,1)S(1)} %pad_maximum_fusion) | data formatting | bytes 589824 | tf_op jit(solution)/shard_map/broadcast_in_dim;reshape | solution.py:211
  98.3 11.3 %all-to-all-done.1 = bf16[64,24,128]{2,1,0:T(8,128)(2,1)S(1)} async-done(((bf16[64,24,128]{2,1,0:T(8,128)(2,1)}), bf16[64,24,128]{2,1,0:T(8,128)(2,1)S(1)}, u32[]{:S(2)}, u32[]{:S(2)}) %all-to-all-start.1) | async-done | bytes 393248 | tf_op jit(solution)/shard_map/all_to_all | solution.py:208
  109.5 0.2 fusion.18
  109.7 0.2 pad_maximum_fusion.1
  109.9 1.5 %broadcast_in_dim_reshape.10 = bf16[1,1,64,2304]{3,2,1,0:T(8,128)(2,1)} reshape(bf16[64,48,48]{2,1,0:T(8,128)(2,1)S(1)} %pad_maximum_fusion.1) | data formatting | bytes 589824 | tf_op jit(solution)/shard_map/broadcast_in_dim;reshape | solution.py:211
  (14 shorter events, 0.1 us)
Async XLA Ops:
  8.6 18.4 %copy-start.2 = (bf16[4,48,128]{2,1,0:T(8,128)(2,1)S(1)}, bf16[4,48,128]{2,1,0:T(8,128)(2,1)}, u32[]{:S(2)}) copy-start(bf16[4,48,128]{2,1,0:T(8,128)(2,1)} %get-tuple-element.6) | copy-start | bytes 147460
  8.6 19.7 %copy-start.1 = (s32[1,1,2,4]{3,2,1,0:T(2,128)S(1)}, s32[1,1,2,4]{3,2,1,0:T(2,128)}, u32[]{:S(2)}) copy-start(s32[1,1,2,4]{3,2,1,0:T(2,128)} %param.16) | copy-start | bytes 100
  8.6 22.9 %copy-start = (bf16[1,1,48,8192]{3,2,1,0:T(8,128)(2,1)S(1)}, bf16[1,1,48,8192]{3,2,1,0:T(8,128)(2,1)}, u32[]{:S(2)}) copy-start(bf16[1,1,48,8192]{3,2,1,0:T(8,128)(2,1)} %param.9) | copy-start | bytes 2359300
  8.6 67.1 %all-to-all-start = ((bf16[64,56,128]{2,1,0:T(8,128)(2,1)}), bf16[64,56,128]{2,1,0:T(8,128)(2,1)S(1)}, u32[]{:S(2)}, u32[]{:S(2)}) async-start(bf16[64,56,128]{2,1,0:T(8,128)(2,1)} %get-tuple-element.5), calls=%async_computation | async-start | bytes 1835008 | tf_op jit(solution)/shard_map/all_to_all | solution.py:180
  27.0 5.2 %collective-permute-start = (bf16[4,48,128]{2,1,0:T(8,128)(2,1)S(1)}, bf16[4,48,128]{2,1,0:T(8,128)(2,1)S(1)}, u32[]{:S(2)}, u32[]{:S(2)}) collective-permute-start(bf16[4,48,128]{2,1,0:T(8,128)(2,1)S(1)} %copy-done.2), channel_id=1, source_target_pairs={{0,64},{64,128},{128,192},{192,256},{256,320},{320,384},{384,448},... | collective-permute-start | bytes 147464 | tf_op jit(solution)/shard_map/ppermute | solution.py:182
  32.5 15.3 %collective-permute-start.1 = (bf16[1,32,128]{2,1,0:T(8,128)(2,1)S(1)}, bf16[1,32,128]{2,1,0:T(8,128)(2,1)S(1)}, u32[]{:S(2)}, u32[]{:S(2)}) collective-permute-start(bf16[1,32,128]{2,1,0:T(8,128)(2,1)S(1)} %get-tuple-element.8), channel_id=1, source_target_pairs={{0,512},{64,576},{128,640},{192,704},{256,768},{320,832},{384,896}... | collective-permute-start | bytes 24584 | tf_op jit(solution)/shard_map/ppermute | solution.py:198
  47.8 12.0 %collective-permute-start.2 = (bf16[2,32,128]{2,1,0:T(8,128)(2,1)S(1)}, bf16[2,32,128]{2,1,0:T(8,128)(2,1)S(1)}, u32[]{:S(2)}, u32[]{:S(2)}) collective-permute-start(bf16[2,32,128]{2,1,0:T(8,128)(2,1)S(1)} %pad_maximum_fusion.5), channel_id=1, source_target_pairs={{0,256},{64,320},{128,384},{192,448},{256,512},{320,576},{384,640}... | collective-permute-start | bytes 49160 | tf_op jit(solution)/shard_map/ppermute | solution.py:198
  59.9 9.2 %collective-permute-start.3 = (bf16[4,32,128]{2,1,0:T(8,128)(2,1)S(1)}, bf16[4,32,128]{2,1,0:T(8,128)(2,1)S(1)}, u32[]{:S(2)}, u32[]{:S(2)}) collective-permute-start(bf16[4,32,128]{2,1,0:T(8,128)(2,1)S(1)} %pad_maximum_fusion.3), channel_id=1, source_target_pairs={{0,128},{64,192},{128,256},{192,320},{256,384},{320,448},{384,512}... | collective-permute-start | bytes 98312 | tf_op jit(solution)/shard_map/ppermute | solution.py:198
  69.1 6.2 %collective-permute-start.4 = (bf16[8,32,128]{2,1,0:T(8,128)(2,1)S(1)}, bf16[8,32,128]{2,1,0:T(8,128)(2,1)S(1)}, u32[]{:S(2)}, u32[]{:S(2)}) collective-permute-start(bf16[8,32,128]{2,1,0:T(8,128)(2,1)S(1)} %pad_maximum_fusion.2), channel_id=1, source_target_pairs={{0,64},{64,128},{128,192},{192,256},{256,320},{320,384},{384,448},... | collective-permute-start | bytes 196616 | tf_op jit(solution)/shard_map/ppermute | solution.py:198
  79.9 29.6 %all-to-all-start.1 = ((bf16[64,24,128]{2,1,0:T(8,128)(2,1)}), bf16[64,24,128]{2,1,0:T(8,128)(2,1)S(1)}, u32[]{:S(2)}, u32[]{:S(2)}) async-start(bf16[64,24,128]{2,1,0:T(8,128)(2,1)} %coupling_blocks.1), calls=%async_computation.1 | async-start | bytes 786432 | tf_op jit(solution)/shard_map/all_to_all | solution.py:208

commit v2 on v1

--- a/solution.py
+++ b/solution.py
@@ -1,3 +1,5 @@
+import math
+
 import jax
 import jax.numpy as jnp
 from jax import lax
@@ -115,17 +117,11 @@
     copy.start()
     copy.wait()
     gap = jnp.zeros((HALF_LANES - vectors, LANES), jnp.bfloat16)
-    left = lax.broadcasted_iota(jnp.int32, (half, LANES), 1) < HALF_LANES
-
-    def one(s, carry):
+    for s in range(partners):
         start = pl.multiple_of(landing_ref[s, 0] * LANES, LANES)
-        tile = basis_ref[:, pl.ds(start, LANES)]
-        twice = jnp.concatenate([tile, gap, tile, gap], axis=0)
-        block = dot_nt(arrived_ref[s, 0:vectors, :], twice)
-        packed_ref[s] = jnp.where(left, block[:half], block[half:]).astype(jnp.bfloat16)
-        return carry
-
-    lax.fori_loop(0, partners, one, 0, unroll=8)
+        tile = jnp.concatenate([basis_ref[:, pl.ds(start, LANES)], gap], axis=0)
+        block = dot_nt(arrived_ref[s, 0:vectors, :], tile)
+        packed_ref[s] = jnp.concatenate([block[:half], block[half:]], axis=1).astype(jnp.bfloat16)
 
 
 def coupling_blocks(arrived, basis):
@@ -145,11 +141,70 @@
     )(arrived, basis)
 
 
+def flatten_into(packed_ref, rows_ref, flat_ref):
+    partners, half, _ = packed_ref.shape
+    vectors = 2 * half
+    rows_ref[...] = packed_ref[...].astype(jnp.float32).reshape(partners * half, LANES)
+    lane = lax.broadcasted_iota(jnp.int32, (partners, LANES), 1)
+    columns = {}
+    for k in range(vectors):
+        side, row = divmod(k, half)
+        value = rows_ref[pl.ds(row, partners, stride=half), :]
+        column, offset = divmod(k * vectors, LANES)
+        shift = (offset - side * HALF_LANES) % LANES
+        if shift:
+            value = pltpu.roll(value, shift, 1)
+        for at, low, high in (
+            (column, offset, min(offset + vectors, LANES)),
+            (column + 1, 0, offset + vectors - LANES),
+        ):
+            if high > low:
+                inside = (lane >= low) & (lane < high)
+                columns[at] = jnp.where(inside, value, columns[at]) if at in columns else value
+        for at in range(column, (k + 1) * vectors // LANES):
+            flat_ref[:, at * LANES : (at + 1) * LANES] = columns.pop(at).astype(jnp.bfloat16)
+
+
+def flat_kernel(packed_ref, flat_ref, rows_ref):
+    flatten_into(packed_ref, rows_ref, flat_ref)
+
+
+def flat_relay_kernel(packed_ref, relay_ref, flat_ref, relayed_ref, rows_ref):
+    flatten_into(packed_ref, rows_ref, flat_ref)
+    relayed_ref[...] = relay_ref[...]
+
+
+def flattened(packed, relay=None):
+    partners, half, _ = packed.shape
+    operands = (packed,) if relay is None else (packed, relay)
+    flat = jax.ShapeDtypeStruct((partners, 4 * half * half), jnp.bfloat16)
+    shapes = flat if relay is None else (flat, jax.ShapeDtypeStruct(relay.shape, relay.dtype))
+    whole = pl.BlockSpec(memory_space=pltpu.VMEM)
+    return pl.pallas_call(
+        flat_kernel if relay is None else flat_relay_kernel,
+        out_shape=shapes,
+        in_specs=[whole] * len(operands),
+        out_specs=whole if relay is None else (whole, whole),
+        scratch_shapes=[pltpu.VMEM((partners * half, LANES), jnp.float32)],
+        compiler_params=pltpu.CompilerParams(vmem_limit_bytes=32 * 1024 * 1024),
+        name="flatten" if relay is None else "flatten_relay",
+    )(*operands)
+
+
 def unpack(packed, vectors):
     both = jnp.concatenate(
         [packed[..., :vectors], packed[..., HALF_LANES : HALF_LANES + vectors]], axis=-2
     )
     return both.reshape(both.shape[:-2] + (vectors * vectors,))
+
+
+def exchanged(blocks, steps):
+    groups = lax.axis_size("grp")
+    others = [
+        lax.ppermute(blocks, "grp", [(g, (g + step) % groups) for g in range(groups)])
+        for step in steps
+    ]
+    return jnp.concatenate([blocks, *others], axis=0)
 
 
 def per_device(
@@ -188,26 +243,22 @@
     )
     face = jnp.einsum("jki,jli->kl", incoming, own, preferred_element_type=jnp.float32)
     half = vectors // 2
-    pad = jnp.zeros((half, HALF_LANES - vectors), jnp.bfloat16)
+    owner = jnp.full((half, HALF_LANES - vectors), owner_map[0], jnp.int32).astype(jnp.bfloat16)
     small = face.astype(jnp.bfloat16)
-    small = jnp.concatenate([small[:half], pad, small[half:], pad], axis=1)
-    owner = jnp.full((INDEX_ROWS, LANES), owner_map[0], jnp.int32).astype(jnp.bfloat16)
-    gathered = jnp.concatenate([small, owner], axis=0)[None]
-    step = groups // 2
-    while step >= 1:
-        other = lax.ppermute(gathered, "grp", [(g, (g + step) % groups) for g in range(groups)])
-        gathered = jnp.concatenate([gathered, other], axis=0)
-        step //= 2
-    mine = gathered[:, half, 0] == lax.axis_index("grp").astype(jnp.bfloat16)
-    owned = jnp.sum(
-        jnp.where(mine[:, None, None], gathered[:, :half].astype(jnp.float32), 0.0), axis=0
-    )
-    owned = unpack(owned, vectors)[None, None]
+    small = jnp.concatenate([small[:half], owner, small[half:], owner], axis=1)[None]
+    stride = math.isqrt(groups)
+    near = exchanged(small, [stride * i for i in range(1, groups // stride)])
 
     packed = coupling_blocks(arrived, basis_rows)
     returned = lax.all_to_all(packed, "sub", split_axis=0, concat_axis=0, tiled=True)
-    coupling_in = unpack(packed, vectors)
-    coupling_out = unpack(returned, vectors)
+    coupling_in, near = flattened(packed, near)
+    faces = exchanged(near, range(1, stride))
+    mine = faces[:, 0, vectors] == lax.axis_index("grp").astype(jnp.bfloat16)
+    owned = jnp.sum(
+        jnp.where(mine[:, None, None], faces.astype(jnp.float32), 0.0), axis=0
+    )
+    owned = unpack(owned, vectors)[None, None]
+    coupling_out = flattened(returned)
     return (coupling_in[None, None], coupling_out[None, None], owned)
 
 

time: 112 us -> 103 us (0.920)
  waiting for transfers between devices: 27.7 us -> 18.6 us
  local copies, waits for them, and re-layouts: 5.88 us -> 1.5 us
  starting transfers between devices: 60.5 us -> 64 us
  Pallas kernels: 12.1 us -> 13.6 us
    ppermute x4 -> x6, waiting for transfers between devices: 16.4 us -> 4.89 us  [exchanged(): lax.ppermute(blocks, 'grp', [(g, (g + step) % groups) for g in range(grou...]
    ppermute x4 -> x6, starting transfers between devices: 26.3 us -> 31.9 us  [exchanged(): lax.ppermute(blocks, 'grp', [(g, (g + step) % groups) for g in range(grou...]
    pallas_call x0 -> x2, Pallas kernels: none -> 3.09 us  [flattened(): pl.pallas_call(flat_kernel if relay is None else flat_relay_kernel, out_s...]
    another operation x2 -> x0, local copies, waits for them, and re-layouts: 2.96 us -> none  [per_device(): return (coupling_in[None, None], coupling_out[None, None], owned)]
    all_to_all x1, waiting for transfers between devices: 11.3 us -> 13.7 us  [per_device(): lax.all_to_all(packed, 'sub', split_axis=0, concat_axis=0, tiled=True)]
    all_to_all x1, starting transfers between devices: 14.6 us -> 12.6 us  [per_device(): lax.all_to_all(packed, 'sub', split_axis=0, concat_axis=0, tiled=True)]
    pallas_call x1, Pallas kernels: 4.15 us -> 2.55 us  [coupling_blocks(): pl.pallas_call(block_kernel, out_shape=jax.ShapeDtypeStruct((partners, ba...]
    slice x3 -> x1, local copies, waits for them, and re-layouts: 1.53 us -> 0.07 us  [unpack(): packed[..., :vectors]]
  transfers between devices with their start and end apart: 7 -> 9, of which waited for: 5 -> 2; matrix products, arithmetic and copies ran while one was open for 5% -> 2% of each run, Pallas kernels for 0% -> 0%
where the time goes in v2:
time: 103 us
  starting transfers between devices  64 us (62%)
  waiting for transfers between devices  18.6 us (18%)
  Pallas kernels  13.6 us (13%)
  between operations  4.09 us (4%)
  local copies, waits for them, and re-layouts  1.5 us (1%)
    ppermute x6, starting transfers between devices, exchanged(): lax.ppermute(blocks, 'grp', [(g, (g + step) % groups) for g in range(grou...  31.9 us
    all_to_all x1, starting transfers between devices, per_device(): lax.all_to_all(payload, 'sub', split_axis=0, concat_axis=0, tiled=True)  18.2 us
    all_to_all x1, waiting for transfers between devices, per_device(): lax.all_to_all(packed, 'sub', split_axis=0, concat_axis=0, tiled=True)  13.7 us
    all_to_all x1, starting transfers between devices, per_device(): lax.all_to_all(packed, 'sub', split_axis=0, concat_axis=0, tiled=True)  12.6 us
    pallas_call x1, Pallas kernels, schur_tiles(): pl.pallas_call(schur_kernel, out_shape=(jax.ShapeDtypeStruct((partners, v...  8 us
    ppermute x6, waiting for transfers between devices, exchanged(): lax.ppermute(blocks, 'grp', [(g, (g + step) % groups) for g in range(grou...  4.89 us
    pallas_call x2, Pallas kernels, flattened(): pl.pallas_call(flat_kernel if relay is None else flat_relay_kernel, out_s...  3.09 us
    pallas_call x1, Pallas kernels, coupling_blocks(): pl.pallas_call(block_kernel, out_shape=jax.ShapeDtypeStruct((partners, ba...  2.55 us
  transfers between devices with their start and end apart: 9, of which 2 were waited for; matrix products, arithmetic and copies ran while one was open for 2% of the time, Pallas kernels for 0%

profile of v2, /device:TPU:1, one launch (start us, length us, event | category | flops | bytes accessed | tf_op | source)
XLA Modules:
  0.0 102.5 jit_solution(15967995258666605076)
XLA Ops:
  0.6 0.0 copy-start
  0.6 0.0 copy-start.1
  0.7 8.0 %schur_tiles.1 = (bf16[64,56,128]{2,1,0:T(8,128)(2,1)}, bf16[4,48,128]{2,1,0:T(8,128)(2,1)}) custom-call(bf16[48,8192]{1,0:T(8,128)(2,1)} %bitcast.30, f32[1,8192]{1,0:T(1,128)} %bitcast.34, bf16[8192,512]{1,0:T(8,128)(2,1)} %bitcast.32, bf16[64,128]{1,0:T(8,128)(2,1)} %bitcast.35, s32[1,64]{1,0:T(1,128)} %bitcast.37, s32[1,64]{1,0:T(1,128)} %bitcast.38, ...), custom_call_target="tpu_custom_call" | custom-call | tf_op jit(solution)/shard_map/schur_tiles/pallas_call | solution.py:83
  8.7 18.2 %all-to-all-start = ((bf16[64,56,128]{2,1,0:T(8,128)(2,1)}), bf16[64,56,128]{2,1,0:T(8,128)(2,1)S(1)}, u32[]{:S(2)}, u32[]{:S(2)}) async-start(bf16[64,56,128]{2,1,0:T(8,128)(2,1)} %get-tuple-element.7), calls=%async_computation | async-start | bytes 1835008 | tf_op jit(solution)/shard_map/all_to_all | solution.py:235
  26.9 1.3 %collective-permute-start = (bf16[4,48,128]{2,1,0:T(8,128)(2,1)}, bf16[4,48,128]{2,1,0:T(8,128)(2,1)S(1)}, u32[]{:S(2)}, u32[]{:S(2)}) collective-permute-start(bf16[4,48,128]{2,1,0:T(8,128)(2,1)} %get-tuple-element.8), channel_id=1, source_target_pairs={{0,64},{64,128},{128,192},{192,256},{256,320},{320,384},{384,448},... | collective-permute-start | bytes 147464 | tf_op jit(solution)/shard_map/ppermute | solution.py:237
  28.2 0.7 fusion.11
  31.4 0.0 copy-done
  32.1 0.0 collective-permute-done
  32.1 0.1 fusion
  32.3 0.1 maximum_bitcast_fusion
  32.4 6.7 %collective-permute-start.1 = (bf16[1,24,128]{2,1,0:T(8,128)(2,1)S(1)}, bf16[1,24,128]{2,1,0:T(8,128)(2,1)S(1)}, u32[]{:S(2)}, u32[]{:S(2)}) collective-permute-start(bf16[1,24,128]{2,1,0:T(8,128)(2,1)S(1)} %maximum_bitcast_fusion), channel_id=1, source_target_pairs={{0,256},{64,320},{128,384},{192,448},{256,512},{320,576},{384,640}... | collective-permute-start | bytes 18440 | tf_op jit(solution)/shard_map/ppermute | solution.py:204
  39.1 13.4 %collective-permute-start.2 = (bf16[1,24,128]{2,1,0:T(8,128)(2,1)S(1)}, bf16[1,24,128]{2,1,0:T(8,128)(2,1)S(1)}, u32[]{:S(2)}, u32[]{:S(2)}) collective-permute-start(bf16[1,24,128]{2,1,0:T(8,128)(2,1)S(1)} %maximum_bitcast_fusion), channel_id=1, source_target_pairs={{0,512},{64,576},{128,640},{192,704},{256,768},{320,832},{384,896}... | collective-permute-start | bytes 18440 | tf_op jit(solution)/shard_map/ppermute | solution.py:204
  52.5 3.4 %collective-permute-start.3 = (bf16[1,24,128]{2,1,0:T(8,128)(2,1)S(1)}, bf16[1,24,128]{2,1,0:T(8,128)(2,1)S(1)}, u32[]{:S(2)}, u32[]{:S(2)}) collective-permute-start(bf16[1,24,128]{2,1,0:T(8,128)(2,1)S(1)} %maximum_bitcast_fusion), channel_id=1, source_target_pairs={{0,768},{64,832},{128,896},{192,960},{256,0},{320,64},{384,128},{4... | collective-permute-start | bytes 18440 | tf_op jit(solution)/shard_map/ppermute | solution.py:204
  55.9 0.0 collective-permute-done.1
  55.9 0.0 collective-permute-done.2
  55.9 4.9 %collective-permute-done.3 = bf16[1,24,128]{2,1,0:T(8,128)(2,1)S(1)} collective-permute-done((bf16[1,24,128]{2,1,0:T(8,128)(2,1)S(1)}, bf16[1,24,128]{2,1,0:T(8,128)(2,1)S(1)}, u32[]{:S(2)}, u32[]{:S(2)}) %collective-permute-start.3) | collective-permute-done | bytes 6176 | tf_op jit(solution)/shard_map/ppermute | solution.py:204
  60.8 0.0 all-to-all-done.arrived_ref
  60.8 2.6 %coupling_blocks.1.packed_ref = bf16[64,24,128]{2,1,0:T(8,128)(2,1)} custom-call(bf16[64,56,128]{2,1,0:T(8,128)(2,1)S(1)} %all-to-all-done.arrived_ref, bf16[48,8192]{1,0:T(8,128)(2,1)S(1)} %bitcast.31), custom_call_target="tpu_custom_call" | custom-call | tf_op jit(solution)/shard_map/coupling_blocks/pallas_call | solution.py:129
  63.4 2.0 %flatten_relay.1 = (bf16[64,2304]{1,0:T(8,128)(2,1)}, bf16[4,24,128]{2,1,0:T(8,128)(2,1)S(1)}) custom-call(bf16[64,24,128]{2,1,0:T(8,128)(2,1)} %coupling_blocks.1.packed_ref, bf16[4,24,128]{2,1,0:T(8,128)(2,1)S(1)} %pad_maximum_fusion.relay_ref), custom_call_target="tpu_custom_call" | custom-call | tf_op jit(solution)/shard_map/flatten_relay/pallas_call | solution.py:183
  65.4 3.1 %collective-permute-start.4 = (bf16[4,24,128]{2,1,0:T(8,128)(2,1)S(1)}, bf16[4,24,128]{2,1,0:T(8,128)(2,1)S(1)}, u32[]{:S(2)}, u32[]{:S(2)}) collective-permute-start(bf16[4,24,128]{2,1,0:T(8,128)(2,1)S(1)} %get-tuple-element.10), channel_id=1, source_target_pairs={{0,64},{64,128},{128,192},{192,256},{256,320},{320,384},{384,448},... | collective-permute-start | bytes 73736 | tf_op jit(solution)/shard_map/ppermute | solution.py:204
  68.5 2.8 %collective-permute-start.5 = (bf16[4,24,128]{2,1,0:T(8,128)(2,1)S(1)}, bf16[4,24,128]{2,1,0:T(8,128)(2,1)S(1)}, u32[]{:S(2)}, u32[]{:S(2)}) collective-permute-start(bf16[4,24,128]{2,1,0:T(8,128)(2,1)S(1)} %get-tuple-element.10), channel_id=1, source_target_pairs={{0,128},{64,192},{128,256},{192,320},{256,384},{320,448},{384,512}... | collective-permute-start | bytes 73736 | tf_op jit(solution)/shard_map/ppermute | solution.py:204
  71.4 2.5 %collective-permute-start.6 = (bf16[4,24,128]{2,1,0:T(8,128)(2,1)S(1)}, bf16[4,24,128]{2,1,0:T(8,128)(2,1)S(1)}, u32[]{:S(2)}, u32[]{:S(2)}) collective-permute-start(bf16[4,24,128]{2,1,0:T(8,128)(2,1)S(1)} %get-tuple-element.10), channel_id=1, source_target_pairs={{0,192},{64,256},{128,320},{192,384},{256,448},{320,512},{384,576}... | collective-permute-start | bytes 73736 | tf_op jit(solution)/shard_map/ppermute | solution.py:204
  73.8 12.6 %all-to-all-start.1 = ((bf16[64,24,128]{2,1,0:T(8,128)(2,1)}), bf16[64,24,128]{2,1,0:T(8,128)(2,1)S(1)}, u32[]{:S(2)}, u32[]{:S(2)}) async-start(bf16[64,24,128]{2,1,0:T(8,128)(2,1)} %coupling_blocks.1.packed_ref), calls=%async_computation.1 | async-start | bytes 786432 | tf_op jit(solution)/shard_map/all_to_all | solution.py:253
  86.4 0.0 collective-permute-done.4
  86.4 0.0 collective-permute-done.5
  86.5 0.0 collective-permute-done.6
  86.5 0.4 compare_reduce_fusion
  86.9 0.1 select_reduce_fusion
  87.0 0.1 fusion.9
  87.1 0.7 broadcast_in_dim_reshape.3
  87.8 13.7 %all-to-all-done.1.packed_ref = bf16[64,24,128]{2,1,0:T(8,128)(2,1)S(1)} async-done(((bf16[64,24,128]{2,1,0:T(8,128)(2,1)}), bf16[64,24,128]{2,1,0:T(8,128)(2,1)S(1)}, u32[]{:S(2)}, u32[]{:S(2)}) %all-to-all-start.1) | async-done | bytes 393248 | tf_op jit(solution)/shard_map/all_to_all | solution.py:253
  101.5 1.0 %flatten.1 = bf16[64,2304]{1,0:T(8,128)(2,1)} custom-call(bf16[64,24,128]{2,1,0:T(8,128)(2,1)S(1)} %all-to-all-done.1.packed_ref), custom_call_target="tpu_custom_call" | custom-call | tf_op jit(solution)/shard_map/flatten/pallas_call | solution.py:183
  (10 shorter events, 0.1 us)
Async XLA Ops:
  0.6 30.8 %copy-start = (bf16[1,1,48,8192]{3,2,1,0:T(8,128)(2,1)S(1)}, bf16[1,1,48,8192]{3,2,1,0:T(8,128)(2,1)}, u32[]{:S(2)}) copy-start(bf16[1,1,48,8192]{3,2,1,0:T(8,128)(2,1)} %param.9) | copy-start | bytes 2359300
  0.6 27.6 %copy-start.1 = (s32[1,1,2,4]{3,2,1,0:T(2,128)S(1)}, s32[1,1,2,4]{3,2,1,0:T(2,128)}, u32[]{:S(2)}) copy-start(s32[1,1,2,4]{3,2,1,0:T(2,128)} %param.16) | copy-start | bytes 100
  8.7 52.1 %all-to-all-start = ((bf16[64,56,128]{2,1,0:T(8,128)(2,1)}), bf16[64,56,128]{2,1,0:T(8,128)(2,1)S(1)}, u32[]{:S(2)}, u32[]{:S(2)}) async-start(bf16[64,56,128]{2,1,0:T(8,128)(2,1)} %get-tuple-element.7), calls=%async_computation | async-start | bytes 1835008 | tf_op jit(solution)/shard_map/all_to_all | solution.py:235
  26.9 5.2 %collective-permute-start = (bf16[4,48,128]{2,1,0:T(8,128)(2,1)}, bf16[4,48,128]{2,1,0:T(8,128)(2,1)S(1)}, u32[]{:S(2)}, u32[]{:S(2)}) collective-permute-start(bf16[4,48,128]{2,1,0:T(8,128)(2,1)} %get-tuple-element.8), channel_id=1, source_target_pairs={{0,64},{64,128},{128,192},{192,256},{256,320},{320,384},{384,448},... | collective-permute-start | bytes 147464 | tf_op jit(solution)/shard_map/ppermute | solution.py:237
  32.4 23.5 %collective-permute-start.1 = (bf16[1,24,128]{2,1,0:T(8,128)(2,1)S(1)}, bf16[1,24,128]{2,1,0:T(8,128)(2,1)S(1)}, u32[]{:S(2)}, u32[]{:S(2)}) collective-permute-start(bf16[1,24,128]{2,1,0:T(8,128)(2,1)S(1)} %maximum_bitcast_fusion), channel_id=1, source_target_pairs={{0,256},{64,320},{128,384},{192,448},{256,512},{320,576},{384,640}... | collective-permute-start | bytes 18440 | tf_op jit(solution)/shard_map/ppermute | solution.py:204
  39.1 16.8 %collective-permute-start.2 = (bf16[1,24,128]{2,1,0:T(8,128)(2,1)S(1)}, bf16[1,24,128]{2,1,0:T(8,128)(2,1)S(1)}, u32[]{:S(2)}, u32[]{:S(2)}) collective-permute-start(bf16[1,24,128]{2,1,0:T(8,128)(2,1)S(1)} %maximum_bitcast_fusion), channel_id=1, source_target_pairs={{0,512},{64,576},{128,640},{192,704},{256,768},{320,832},{384,896}... | collective-permute-start | bytes 18440 | tf_op jit(solution)/shard_map/ppermute | solution.py:204
  52.5 8.3 %collective-permute-start.3 = (bf16[1,24,128]{2,1,0:T(8,128)(2,1)S(1)}, bf16[1,24,128]{2,1,0:T(8,128)(2,1)S(1)}, u32[]{:S(2)}, u32[]{:S(2)}) collective-permute-start(bf16[1,24,128]{2,1,0:T(8,128)(2,1)S(1)} %maximum_bitcast_fusion), channel_id=1, source_target_pairs={{0,768},{64,832},{128,896},{192,960},{256,0},{320,64},{384,128},{4... | collective-permute-start | bytes 18440 | tf_op jit(solution)/shard_map/ppermute | solution.py:204
  65.4 21.0 %collective-permute-start.4 = (bf16[4,24,128]{2,1,0:T(8,128)(2,1)S(1)}, bf16[4,24,128]{2,1,0:T(8,128)(2,1)S(1)}, u32[]{:S(2)}, u32[]{:S(2)}) collective-permute-start(bf16[4,24,128]{2,1,0:T(8,128)(2,1)S(1)} %get-tuple-element.10), channel_id=1, source_target_pairs={{0,64},{64,128},{128,192},{192,256},{256,320},{320,384},{384,448},... | collective-permute-start | bytes 73736 | tf_op jit(solution)/shard_map/ppermute | solution.py:204
  68.5 17.9 %collective-permute-start.5 = (bf16[4,24,128]{2,1,0:T(8,128)(2,1)S(1)}, bf16[4,24,128]{2,1,0:T(8,128)(2,1)S(1)}, u32[]{:S(2)}, u32[]{:S(2)}) collective-permute-start(bf16[4,24,128]{2,1,0:T(8,128)(2,1)S(1)} %get-tuple-element.10), channel_id=1, source_target_pairs={{0,128},{64,192},{128,256},{192,320},{256,384},{320,448},{384,512}... | collective-permute-start | bytes 73736 | tf_op jit(solution)/shard_map/ppermute | solution.py:204
  71.4 15.1 %collective-permute-start.6 = (bf16[4,24,128]{2,1,0:T(8,128)(2,1)S(1)}, bf16[4,24,128]{2,1,0:T(8,128)(2,1)S(1)}, u32[]{:S(2)}, u32[]{:S(2)}) collective-permute-start(bf16[4,24,128]{2,1,0:T(8,128)(2,1)S(1)} %get-tuple-element.10), channel_id=1, source_target_pairs={{0,192},{64,256},{128,320},{192,384},{256,448},{320,512},{384,576}... | collective-permute-start | bytes 73736 | tf_op jit(solution)/shard_map/ppermute | solution.py:204
  73.8 27.6 %all-to-all-start.1 = ((bf16[64,24,128]{2,1,0:T(8,128)(2,1)}), bf16[64,24,128]{2,1,0:T(8,128)(2,1)S(1)}, u32[]{:S(2)}, u32[]{:S(2)}) async-start(bf16[64,24,128]{2,1,0:T(8,128)(2,1)} %coupling_blocks.1.packed_ref), calls=%async_computation.1 | async-start | bytes 786432 | tf_op jit(solution)/shard_map/all_to_all | solution.py:253

commit v3 on v2

--- a/solution.py
+++ b/solution.py
@@ -107,7 +107,9 @@
     )(*operands)
 
 
-def block_kernel(arrived_ref, basis_ref, packed_ref, index_ref, landing_ref, sem):
+def block_kernel(
+    arrived_ref, basis_ref, relay_ref, packed_ref, relayed_ref, index_ref, landing_ref, sem
+):
     vectors = basis_ref.shape[0]
     partners = arrived_ref.shape[0]
     half = vectors // 2
@@ -115,6 +117,7 @@
     index_ref[...] = jnp.max(marks, axis=1).astype(jnp.int32)
     copy = pltpu.make_async_copy(index_ref, landing_ref, sem)
     copy.start()
+    relayed_ref[...] = relay_ref[...]
     copy.wait()
     gap = jnp.zeros((HALF_LANES - vectors, LANES), jnp.bfloat16)
     for s in range(partners):
@@ -124,13 +127,16 @@
         packed_ref[s] = jnp.concatenate([block[:half], block[half:]], axis=1).astype(jnp.bfloat16)
 
 
-def coupling_blocks(arrived, basis):
+def coupling_blocks(arrived, basis, relay):
     partners = arrived.shape[0]
     return pl.pallas_call(
         block_kernel,
-        out_shape=jax.ShapeDtypeStruct((partners, basis.shape[0] // 2, LANES), jnp.bfloat16),
-        in_specs=[pl.BlockSpec(memory_space=pltpu.VMEM)] * 2,
-        out_specs=pl.BlockSpec(memory_space=pltpu.VMEM),
+        out_shape=(
+            jax.ShapeDtypeStruct((partners, basis.shape[0] // 2, LANES), jnp.bfloat16),
+            jax.ShapeDtypeStruct(relay.shape, relay.dtype),
+        ),
+        in_specs=[pl.BlockSpec(memory_space=pltpu.VMEM)] * 3,
+        out_specs=[pl.BlockSpec(memory_space=pltpu.VMEM)] * 2,
         scratch_shapes=[
             pltpu.VMEM((partners, LANES), jnp.int32),
             pltpu.SMEM((partners, LANES), jnp.int32),
@@ -138,10 +144,10 @@
         ],
         compiler_params=pltpu.CompilerParams(vmem_limit_bytes=32 * 1024 * 1024),
         name="coupling_blocks",
-    )(arrived, basis)
-
-
-def flatten_into(packed_ref, rows_ref, flat_ref):
+    )(arrived, basis, relay)
+
+
+def flatten_kernel(packed_ref, flat_ref, rows_ref):
     partners, half, _ = packed_ref.shape
     vectors = 2 * half
     rows_ref[...] = packed_ref[...].astype(jnp.float32).reshape(partners * half, LANES)
@@ -165,30 +171,17 @@
             flat_ref[:, at * LANES : (at + 1) * LANES] = columns.pop(at).astype(jnp.bfloat16)
 
 
-def flat_kernel(packed_ref, flat_ref, rows_ref):
-    flatten_into(packed_ref, rows_ref, flat_ref)
-
-
-def flat_relay_kernel(packed_ref, relay_ref, flat_ref, relayed_ref, rows_ref):
-    flatten_into(packed_ref, rows_ref, flat_ref)
-    relayed_ref[...] = relay_ref[...]
-
-
-def flattened(packed, relay=None):
+def flattened(packed):
     partners, half, _ = packed.shape
-    operands = (packed,) if relay is None else (packed, relay)
-    flat = jax.ShapeDtypeStruct((partners, 4 * half * half), jnp.bfloat16)
-    shapes = flat if relay is None else (flat, jax.ShapeDtypeStruct(relay.shape, relay.dtype))
-    whole = pl.BlockSpec(memory_space=pltpu.VMEM)
     return pl.pallas_call(
-        flat_kernel if relay is None else flat_relay_kernel,
-        out_shape=shapes,
-        in_specs=[whole] * len(operands),
-        out_specs=whole if relay is None else (whole, whole),
+        flatten_kernel,
+        out_shape=jax.ShapeDtypeStruct((partners, 4 * half * half), jnp.bfloat16),
+        in_specs=[pl.BlockSpec(memory_space=pltpu.VMEM)],
+        out_specs=pl.BlockSpec(memory_space=pltpu.VMEM),
         scratch_shapes=[pltpu.VMEM((partners * half, LANES), jnp.float32)],
         compiler_params=pltpu.CompilerParams(vmem_limit_bytes=32 * 1024 * 1024),
-        name="flatten" if relay is None else "flatten_relay",
-    )(*operands)
+        name="flatten",
+    )(packed)
 
 
 def unpack(packed, vectors):
@@ -198,13 +191,35 @@
     return both.reshape(both.shape[:-2] + (vectors * vectors,))
 
 
-def exchanged(blocks, steps):
+def owner_sums(block, owner_lane):
     groups = lax.axis_size("grp")
-    others = [
-        lax.ppermute(blocks, "grp", [(g, (g + step) % groups) for g in range(groups)])
-        for step in steps
-    ]
-    return jnp.concatenate([blocks, *others], axis=0)
+    hubs = math.isqrt(groups)
+    first = groups - hubs
+    faces = [block]
+    for shift in range(hubs, groups, hubs):
+        faces.append(lax.ppermute(block, "grp", [(h - shift, h) for h in range(first, groups)]))
+    faces = jnp.concatenate(faces, axis=0)
+    step = hubs // 2
+    while step >= 1:
+        pairs = [(first + h, first + (h ^ step)) for h in range(hubs)]
+        faces = jnp.concatenate([faces, lax.ppermute(faces, "grp", pairs)], axis=0)
+        step //= 2
+    served = lax.axis_index("grp") - hubs * jnp.arange(groups // hubs)
+    mine = faces[None, :, 0, owner_lane] == served[:, None].astype(jnp.bfloat16)
+    return jnp.sum(
+        jnp.where(mine[:, :, None, None], faces[None].astype(jnp.float32), 0.0), axis=1
+    )
+
+
+def handed_back(sums):
+    groups = lax.axis_size("grp")
+    hubs = math.isqrt(groups)
+    first = groups - hubs
+    owned = jnp.where(lax.axis_index("grp") >= first, sums[0], 0.0)
+    for i in range(1, groups // hubs):
+        pairs = [(h, h - hubs * i) for h in range(first, groups)]
+        owned = owned + lax.ppermute(sums[i], "grp", pairs)
+    return owned
 
 
 def per_device(
@@ -246,18 +261,11 @@
     owner = jnp.full((half, HALF_LANES - vectors), owner_map[0], jnp.int32).astype(jnp.bfloat16)
     small = face.astype(jnp.bfloat16)
     small = jnp.concatenate([small[:half], owner, small[half:], owner], axis=1)[None]
-    stride = math.isqrt(groups)
-    near = exchanged(small, [stride * i for i in range(1, groups // stride)])
-
-    packed = coupling_blocks(arrived, basis_rows)
+    sums = owner_sums(small, vectors)
+    packed, sums = coupling_blocks(arrived, basis_rows, sums)
     returned = lax.all_to_all(packed, "sub", split_axis=0, concat_axis=0, tiled=True)
-    coupling_in, near = flattened(packed, near)
-    faces = exchanged(near, range(1, stride))
-    mine = faces[:, 0, vectors] == lax.axis_index("grp").astype(jnp.bfloat16)
-    owned = jnp.sum(
-        jnp.where(mine[:, None, None], faces.astype(jnp.float32), 0.0), axis=0
-    )
-    owned = unpack(owned, vectors)[None, None]
+    owned = unpack(handed_back(sums), vectors)[None, None]
+    coupling_in = flattened(packed)
     coupling_out = flattened(returned)
     return (coupling_in[None, None], coupling_out[None, None], owned)
 

time: 103 us -> 90.3 us (0.88)
  starting transfers between devices: 64 us -> 49.2 us
  waiting for transfers between devices: 18.6 us -> 20.6 us
    ppermute x6 -> x8, waiting for transfers between devices: 4.89 us -> 19 us  [the longest x3 18.3 us: handed_back(): owned = owned + lax.ppermute(sums[i], 'grp', pairs)]
    all_to_all x1, waiting for transfers between devices: 13.7 us -> 0.01 us  [per_device(): lax.all_to_all(packed, 'sub', split_axis=0, concat_axis=0, tiled=True)]
    ppermute x6 -> x8, starting transfers between devices: 31.9 us -> 19.6 us  [the longest x3 15.7 us: owner_sums(): lax.ppermute(block, 'grp', [(h - shift, h) for h in range(first, groups)])]
    all_to_all x1, starting transfers between devices: 12.6 us -> 10.1 us  [per_device(): lax.all_to_all(packed, 'sub', split_axis=0, concat_axis=0, tiled=True)]
    all_to_all x1, waiting for transfers between devices: 0.01 us -> 1.54 us  [per_device(): lax.all_to_all(payload, 'sub', split_axis=0, concat_axis=0, tiled=True)]
  transfers between devices with their start and end apart: 9 -> 11, of which waited for: 2 -> 3; matrix products, arithmetic and copies ran while one was open for 2% -> 3% of each run, Pallas kernels for 0% -> 2%
where the time goes in v3:
time: 90.3 us; the launch traced here: 89.8 us
  starting transfers between devices  49.2 us (54%)
  waiting for transfers between devices  20.6 us (23%)
  Pallas kernels  13.7 us (15%)
  between operations  4.08 us (5%)
  local copies, waits for them, and re-layouts  1.8 us (2%)
    ppermute x3, waiting for transfers between devices, handed_back(): owned = owned + lax.ppermute(sums[i], 'grp', pairs)  18.3 us
    all_to_all x1, starting transfers between devices, per_device(): lax.all_to_all(payload, 'sub', split_axis=0, concat_axis=0, tiled=True)  18.2 us
    ppermute x3, starting transfers between devices, owner_sums(): lax.ppermute(block, 'grp', [(h - shift, h) for h in range(first, groups)])  15.7 us
    all_to_all x1, starting transfers between devices, per_device(): lax.all_to_all(packed, 'sub', split_axis=0, concat_axis=0, tiled=True)  10.1 us
    pallas_call x1, Pallas kernels, schur_tiles(): pl.pallas_call(schur_kernel, out_shape=(jax.ShapeDtypeStruct((partners, v...  8.01 us
    pallas_call x2, Pallas kernels, flattened(): pl.pallas_call(flatten_kernel, out_shape=jax.ShapeDtypeStruct((partners,...  3.09 us
    ppermute x3, starting transfers between devices, handed_back(): owned = owned + lax.ppermute(sums[i], 'grp', pairs)  2.62 us
    pallas_call x1, Pallas kernels, coupling_blocks(): pl.pallas_call(block_kernel, out_shape=(jax.ShapeDtypeStruct((partners, b...  2.56 us
  transfers between devices with their start and end apart: 11, of which 3 were waited for; matrix products, arithmetic and copies ran while one was open for 3% of the time, Pallas kernels for 2%

profile of v3, /device:TPU:1, one launch (start us, length us, event | category | flops | bytes accessed | tf_op | source)
XLA Modules:
  0.0 89.8 jit_solution(7566725697618554548)
XLA Ops:
  0.7 8.0 %schur_tiles.1 = (bf16[64,56,128]{2,1,0:T(8,128)(2,1)}, bf16[4,48,128]{2,1,0:T(8,128)(2,1)}) custom-call(bf16[48,8192]{1,0:T(8,128)(2,1)} %bitcast.43, f32[1,8192]{1,0:T(1,128)} %bitcast.48, bf16[8192,512]{1,0:T(8,128)(2,1)} %bitcast.45, bf16[64,128]{1,0:T(8,128)(2,1)} %bitcast.49, s32[1,64]{1,0:T(1,128)} %bitcast.51, s32[1,64]{1,0:T(1,128)} %bitcast.52, ...), custom_call_target="tpu_custom_call" | custom-call | tf_op jit(solution)/shard_map/schur_tiles/pallas_call | solution.py:83
  8.7 18.2 %all-to-all-start = ((bf16[64,56,128]{2,1,0:T(8,128)(2,1)}), bf16[64,56,128]{2,1,0:T(8,128)(2,1)S(1)}, u32[]{:S(2)}, u32[]{:S(2)}) async-start(bf16[64,56,128]{2,1,0:T(8,128)(2,1)} %get-tuple-element.7), calls=%async_computation | async-start | bytes 1835008 | tf_op jit(solution)/shard_map/all_to_all | solution.py:250
  26.9 1.3 %collective-permute-start = (bf16[4,48,128]{2,1,0:T(8,128)(2,1)}, bf16[4,48,128]{2,1,0:T(8,128)(2,1)S(1)}, u32[]{:S(2)}, u32[]{:S(2)}) collective-permute-start(bf16[4,48,128]{2,1,0:T(8,128)(2,1)} %get-tuple-element.8), channel_id=1, source_target_pairs={{0,64},{64,128},{128,192},{192,256},{256,320},{320,384},{384,448},... | collective-permute-start | bytes 147464 | tf_op jit(solution)/shard_map/ppermute | solution.py:252
  28.2 0.6 fusion.13
  32.1 0.0 collective-permute-done
  32.1 0.1 fusion
  32.2 0.1 constant_dynamic-update-slice_fusion.4
  32.3 0.7 collective-permute-start.1
  33.0 0.7 collective-permute-start.2
  33.7 14.4 %collective-permute-start.3 = (bf16[1,24,128]{2,1,0:T(8,128)(2,1)S(1)}, bf16[1,24,128]{2,1,0:T(8,128)(2,1)S(1)}, u32[]{:S(2)}, u32[]{:S(2)}) collective-permute-start(bf16[1,24,128]{2,1,0:T(8,128)(2,1)S(1)} %get-tuple-element.12), channel_id=1, source_target_pairs={{0,768},{64,832},{128,896},{192,960},{1,769},{65,833},{129,897},{1... | collective-permute-start | bytes 18440 | tf_op jit(solution)/shard_map/ppermute | solution.py:200
  48.0 0.0 collective-permute-done.1
  48.1 0.0 collective-permute-done.2
  48.1 0.7 collective-permute-done.3
  48.8 0.7 collective-permute-start.4
  49.5 0.0 collective-permute-done.4
  49.5 0.7 collective-permute-start.5
  50.2 0.0 collective-permute-done.5
  50.3 0.3 slice_reduce_fusion
  50.6 0.1 broadcast_compare_fusion
  50.6 0.1 select_reduce_fusion.relay_ref
  50.8 1.5 %all-to-all-done.arrived_ref = bf16[64,56,128]{2,1,0:T(8,128)(2,1)S(1)} async-done(((bf16[64,56,128]{2,1,0:T(8,128)(2,1)}), bf16[64,56,128]{2,1,0:T(8,128)(2,1)S(1)}, u32[]{:S(2)}, u32[]{:S(2)}) %all-to-all-start) | async-done | bytes 917536 | tf_op jit(solution)/shard_map/all_to_all | solution.py:250
  52.3 2.6 %coupling_blocks.1 = (bf16[64,24,128]{2,1,0:T(8,128)(2,1)}, f32[4,24,128]{2,1,0:T(8,128)S(1)}) custom-call(bf16[64,56,128]{2,1,0:T(8,128)(2,1)S(1)} %all-to-all-done.arrived_ref, bf16[48,8192]{1,0:T(8,128)(2,1)S(1)} %bitcast.44, f32[4,24,128]{2,1,0:T(8,128)S(1)} %select_reduce_fusion.relay_ref), custom_call_target="tpu_custom_call" | custom-call | tf_op jit(solution)/shard_map/coupling_blocks/pallas_call | solution.py:132
  54.9 10.1 %all-to-all-start.1 = ((bf16[64,24,128]{2,1,0:T(8,128)(2,1)}), bf16[64,24,128]{2,1,0:T(8,128)(2,1)S(1)}, u32[]{:S(2)}, u32[]{:S(2)}) async-start(bf16[64,24,128]{2,1,0:T(8,128)(2,1)} %get-tuple-element.9.packed_ref), calls=%async_computation.1 | async-start | bytes 786432 | tf_op jit(solution)/shard_map/all_to_all | solution.py:266
  65.0 1.3 %collective-permute-start.8 = (f32[24,128]{1,0:T(8,128)S(1)}, f32[24,128]{1,0:T(8,128)S(1)}, u32[]{:S(2)}, u32[]{:S(2)}) collective-permute-start(f32[24,128]{1,0:T(8,128)S(1)} %get-tuple-element.18), channel_id=1, source_target_pairs={{768,0},{832,64},{896,128},{960,192},{769,1},{833,65},{897,129},{9... | collective-permute-start | bytes 36872 | tf_op jit(solution)/shard_map/ppermute | solution.py:221
  66.3 0.7 collective-permute-start.7
  67.0 0.7 collective-permute-start.6
  67.6 2.0 %flatten.2 = bf16[64,2304]{1,0:T(8,128)(2,1)} custom-call(bf16[64,24,128]{2,1,0:T(8,128)(2,1)} %get-tuple-element.9.packed_ref), custom_call_target="tpu_custom_call" | custom-call | tf_op jit(solution)/shard_map/flatten/pallas_call | solution.py:176
  69.7 18.3 %collective-permute-done.8 = f32[24,128]{1,0:T(8,128)S(1)} collective-permute-done((f32[24,128]{1,0:T(8,128)S(1)}, f32[24,128]{1,0:T(8,128)S(1)}, u32[]{:S(2)}, u32[]{:S(2)}) %collective-permute-start.8) | collective-permute-done | bytes 12320 | tf_op jit(solution)/shard_map/ppermute | solution.py:221
  88.0 0.0 collective-permute-done.7
  88.0 0.1 fusion.11
  88.1 0.7 broadcast_in_dim_reshape.3
  88.8 1.0 %flatten.3 = bf16[64,2304]{1,0:T(8,128)(2,1)} custom-call(bf16[64,24,128]{2,1,0:T(8,128)(2,1)S(1)} %all-to-all-done.1.packed_ref), custom_call_target="tpu_custom_call" | custom-call | tf_op jit(solution)/shard_map/flatten/pallas_call | solution.py:176
  (21 shorter events, 0.2 us)
Async XLA Ops:
  0.6 30.7 %copy-start = (bf16[1,1,48,8192]{3,2,1,0:T(8,128)(2,1)S(1)}, bf16[1,1,48,8192]{3,2,1,0:T(8,128)(2,1)}, u32[]{:S(2)}) copy-start(bf16[1,1,48,8192]{3,2,1,0:T(8,128)(2,1)} %param.9) | copy-start | bytes 2359300
  0.6 27.6 %copy-start.1 = (s32[1,1,2,4]{3,2,1,0:T(2,128)S(1)}, s32[1,1,2,4]{3,2,1,0:T(2,128)}, u32[]{:S(2)}) copy-start(s32[1,1,2,4]{3,2,1,0:T(2,128)} %param.16) | copy-start | bytes 100
  8.7 43.7 %all-to-all-start = ((bf16[64,56,128]{2,1,0:T(8,128)(2,1)}), bf16[64,56,128]{2,1,0:T(8,128)(2,1)S(1)}, u32[]{:S(2)}, u32[]{:S(2)}) async-start(bf16[64,56,128]{2,1,0:T(8,128)(2,1)} %get-tuple-element.7), calls=%async_computation | async-start | bytes 1835008 | tf_op jit(solution)/shard_map/all_to_all | solution.py:250
  26.9 5.1 %collective-permute-start = (bf16[4,48,128]{2,1,0:T(8,128)(2,1)}, bf16[4,48,128]{2,1,0:T(8,128)(2,1)S(1)}, u32[]{:S(2)}, u32[]{:S(2)}) collective-permute-start(bf16[4,48,128]{2,1,0:T(8,128)(2,1)} %get-tuple-element.8), channel_id=1, source_target_pairs={{0,64},{64,128},{128,192},{192,256},{256,320},{320,384},{384,448},... | collective-permute-start | bytes 147464 | tf_op jit(solution)/shard_map/ppermute | solution.py:252
  32.3 15.7 %collective-permute-start.1 = (bf16[1,24,128]{2,1,0:T(8,128)(2,1)S(1)}, bf16[1,24,128]{2,1,0:T(8,128)(2,1)S(1)}, u32[]{:S(2)}, u32[]{:S(2)}) collective-permute-start(bf16[1,24,128]{2,1,0:T(8,128)(2,1)S(1)} %get-tuple-element.12), channel_id=1, source_target_pairs={{512,768},{576,832},{640,896},{704,960},{513,769},{577,833},{641,8... | collective-permute-start | bytes 18440 | tf_op jit(solution)/shard_map/ppermute | solution.py:200
  33.0 15.1 %collective-permute-start.2 = (bf16[1,24,128]{2,1,0:T(8,128)(2,1)S(1)}, bf16[1,24,128]{2,1,0:T(8,128)(2,1)S(1)}, u32[]{:S(2)}, u32[]{:S(2)}) collective-permute-start(bf16[1,24,128]{2,1,0:T(8,128)(2,1)S(1)} %get-tuple-element.12), channel_id=1, source_target_pairs={{256,768},{320,832},{384,896},{448,960},{257,769},{321,833},{385,8... | collective-permute-start | bytes 18440 | tf_op jit(solution)/shard_map/ppermute | solution.py:200
  33.7 15.1 %collective-permute-start.3 = (bf16[1,24,128]{2,1,0:T(8,128)(2,1)S(1)}, bf16[1,24,128]{2,1,0:T(8,128)(2,1)S(1)}, u32[]{:S(2)}, u32[]{:S(2)}) collective-permute-start(bf16[1,24,128]{2,1,0:T(8,128)(2,1)S(1)} %get-tuple-element.12), channel_id=1, source_target_pairs={{0,768},{64,832},{128,896},{192,960},{1,769},{65,833},{129,897},{1... | collective-permute-start | bytes 18440 | tf_op jit(solution)/shard_map/ppermute | solution.py:200
  48.8 0.7 collective-permute-start.4
  49.5 0.7 collective-permute-start.5
  54.9 33.9 %all-to-all-start.1 = ((bf16[64,24,128]{2,1,0:T(8,128)(2,1)}), bf16[64,24,128]{2,1,0:T(8,128)(2,1)S(1)}, u32[]{:S(2)}, u32[]{:S(2)}) async-start(bf16[64,24,128]{2,1,0:T(8,128)(2,1)} %get-tuple-element.9.packed_ref), calls=%async_computation.1 | async-start | bytes 786432 | tf_op jit(solution)/shard_map/all_to_all | solution.py:266
  65.0 23.0 %collective-permute-start.8 = (f32[24,128]{1,0:T(8,128)S(1)}, f32[24,128]{1,0:T(8,128)S(1)}, u32[]{:S(2)}, u32[]{:S(2)}) collective-permute-start(f32[24,128]{1,0:T(8,128)S(1)} %get-tuple-element.18), channel_id=1, source_target_pairs={{768,0},{832,64},{896,128},{960,192},{769,1},{833,65},{897,129},{9... | collective-permute-start | bytes 36872 | tf_op jit(solution)/shard_map/ppermute | solution.py:221
  66.3 21.7 %collective-permute-start.7 = (f32[24,128]{1,0:T(8,128)S(1)}, f32[24,128]{1,0:T(8,128)S(1)}, u32[]{:S(2)}, u32[]{:S(2)}) collective-permute-start(f32[24,128]{1,0:T(8,128)S(1)} %get-tuple-element.19), channel_id=1, source_target_pairs={{768,256},{832,320},{896,384},{960,448},{769,257},{833,321},{897,3... | collective-permute-start | bytes 36872 | tf_op jit(solution)/shard_map/ppermute | solution.py:221
  67.0 21.0 %collective-permute-start.6 = (f32[24,128]{1,0:T(8,128)S(1)}, f32[24,128]{1,0:T(8,128)S(1)}, u32[]{:S(2)}, u32[]{:S(2)}) collective-permute-start(f32[24,128]{1,0:T(8,128)S(1)} %get-tuple-element.17), channel_id=1, source_target_pairs={{768,512},{832,576},{896,640},{960,704},{769,513},{833,577},{897,6... | collective-permute-start | bytes 36872 | tf_op jit(solution)/shard_map/ppermute | solution.py:221

commit v4 on v3

--- a/solution.py
+++ b/solution.py
@@ -19,7 +19,7 @@
 
 def schur_kernel(
     basis_hbm, bdiag_hbm, interior_hbm, weight_hbm, send_hbm, count_hbm, land_hbm, face_hbm,
-    payload_ref, faces_ref,
+    owner_ref, payload_ref, faces_ref, own_ref,
     basis_ref, bdiag_ref, interior_ref, weight_ref, send_ref, count_ref, land_ref, face_ref,
     tiles_ref, scaled_ref, sems, small_sems,
 ):
@@ -74,9 +74,13 @@
     lax.fori_loop(0, partners, one, 0, unroll=4)
     for j in range(faces_ref.shape[0]):
         faces_ref[j] = tiles_ref[face_ref[1, j]]
-
-
-def schur_tiles(basis, bdiag, interior, weights, send, counts, land, face):
+        start = pl.multiple_of(face_ref[0, j] * LANES, LANES)
+        own_ref[j] = basis_ref[:, pl.ds(start, LANES)]
+    owner = jnp.full((vectors, LANES), owner_ref[0].astype(jnp.float32), jnp.float32)
+    own_ref[faces_ref.shape[0]] = owner.astype(jnp.bfloat16)
+
+
+def schur_tiles(basis, bdiag, interior, weights, send, counts, land, face, owner):
     vectors, interface = basis.shape
     partners = weights.shape[0]
     operands = (basis, bdiag, interior, weights, send, counts, land, face)
@@ -85,9 +89,11 @@
         out_shape=(
             jax.ShapeDtypeStruct((partners, vectors + INDEX_ROWS, LANES), jnp.bfloat16),
             jax.ShapeDtypeStruct((face.shape[1], vectors, LANES), jnp.bfloat16),
+            jax.ShapeDtypeStruct((face.shape[1] + 1, vectors, LANES), jnp.bfloat16),
         ),
-        in_specs=[pl.BlockSpec(memory_space=pltpu.HBM)] * len(operands),
-        out_specs=[pl.BlockSpec(memory_space=pltpu.VMEM)] * 2,
+        in_specs=[pl.BlockSpec(memory_space=pltpu.HBM)] * len(operands)
+        + [pl.BlockSpec(memory_space=pltpu.SMEM)],
+        out_specs=[pl.BlockSpec(memory_space=pltpu.VMEM)] * 3,
         scratch_shapes=[
             pltpu.VMEM(basis.shape, basis.dtype),
             pltpu.VMEM(bdiag.shape, bdiag.dtype),
@@ -104,11 +110,11 @@
         ],
         compiler_params=pltpu.CompilerParams(vmem_limit_bytes=60 * 1024 * 1024),
         name="schur_tiles",
-    )(*operands)
+    )(*operands, owner)
 
 
 def block_kernel(
-    arrived_ref, basis_ref, relay_ref, packed_ref, relayed_ref, index_ref, landing_ref, sem
+    arrived_ref, basis_ref, packed_ref, flat_ref, index_ref, landing_ref, rows_ref, sem
 ):
     vectors = basis_ref.shape[0]
     partners = arrived_ref.shape[0]
@@ -117,40 +123,49 @@
     index_ref[...] = jnp.max(marks, axis=1).astype(jnp.int32)
     copy = pltpu.make_async_copy(index_ref, landing_ref, sem)
     copy.start()
-    relayed_ref[...] = relay_ref[...]
     copy.wait()
     gap = jnp.zeros((HALF_LANES - vectors, LANES), jnp.bfloat16)
     for s in range(partners):
         start = pl.multiple_of(landing_ref[s, 0] * LANES, LANES)
         tile = jnp.concatenate([basis_ref[:, pl.ds(start, LANES)], gap], axis=0)
         block = dot_nt(arrived_ref[s, 0:vectors, :], tile)
-        packed_ref[s] = jnp.concatenate([block[:half], block[half:]], axis=1).astype(jnp.bfloat16)
-
-
-def coupling_blocks(arrived, basis, relay):
+        rows = jnp.concatenate([block[:half], block[half:]], axis=1)
+        packed_ref[s] = rows.astype(jnp.bfloat16)
+        rows_ref[s * half : (s + 1) * half, :] = rows
+    flatten_rows(rows_ref, flat_ref)
+
+
+def coupling_blocks(arrived, basis):
     partners = arrived.shape[0]
+    half = basis.shape[0] // 2
     return pl.pallas_call(
         block_kernel,
         out_shape=(
-            jax.ShapeDtypeStruct((partners, basis.shape[0] // 2, LANES), jnp.bfloat16),
-            jax.ShapeDtypeStruct(relay.shape, relay.dtype),
+            jax.ShapeDtypeStruct((partners, half, LANES), jnp.bfloat16),
+            jax.ShapeDtypeStruct((partners, 4 * half * half), jnp.bfloat16),
         ),
-        in_specs=[pl.BlockSpec(memory_space=pltpu.VMEM)] * 3,
+        in_specs=[pl.BlockSpec(memory_space=pltpu.VMEM)] * 2,
         out_specs=[pl.BlockSpec(memory_space=pltpu.VMEM)] * 2,
         scratch_shapes=[
             pltpu.VMEM((partners, LANES), jnp.int32),
             pltpu.SMEM((partners, LANES), jnp.int32),
+            pltpu.VMEM((partners * half, LANES), jnp.float32),
             pltpu.SemaphoreType.DMA,
         ],
         compiler_params=pltpu.CompilerParams(vmem_limit_bytes=32 * 1024 * 1024),
         name="coupling_blocks",
-    )(arrived, basis, relay)
+    )(arrived, basis)
 
 
 def flatten_kernel(packed_ref, flat_ref, rows_ref):
-    partners, half, _ = packed_ref.shape
+    rows_ref[...] = packed_ref[...].astype(jnp.float32).reshape(rows_ref.shape)
+    flatten_rows(rows_ref, flat_ref)
+
+
+def flatten_rows(rows_ref, flat_ref):
+    partners = flat_ref.shape[0]
+    half = rows_ref.shape[0] // partners
     vectors = 2 * half
-    rows_ref[...] = packed_ref[...].astype(jnp.float32).reshape(partners * half, LANES)
     lane = lax.broadcasted_iota(jnp.int32, (partners, LANES), 1)
     columns = {}
     for k in range(vectors):
@@ -168,7 +183,7 @@
                 inside = (lane >= low) & (lane < high)
                 columns[at] = jnp.where(inside, value, columns[at]) if at in columns else value
         for at in range(column, (k + 1) * vectors // LANES):
-            flat_ref[:, at * LANES : (at + 1) * LANES] = columns.pop(at).astype(jnp.bfloat16)
+            flat_ref[:, at * LANES : (at + 1) * LANES] = columns.pop(at).astype(flat_ref.dtype)
 
 
 def flattened(packed):
@@ -184,11 +199,28 @@
     )(packed)
 
 
-def unpack(packed, vectors):
-    both = jnp.concatenate(
-        [packed[..., :vectors], packed[..., HALF_LANES : HALF_LANES + vectors]], axis=-2
-    )
-    return both.reshape(both.shape[:-2] + (vectors * vectors,))
+def face_kernel(lower_ref, upper_ref, packed_ref):
+    half, vectors = packed_ref.shape[1], lower_ref.shape[1]
+    count = lower_ref.shape[0]
+    gap = jnp.zeros((HALF_LANES - vectors, LANES), jnp.bfloat16)
+    block = jnp.zeros((vectors, HALF_LANES), jnp.float32)
+    for j in range(count):
+        block += dot_nt(lower_ref[j], jnp.concatenate([upper_ref[j], gap], axis=0))
+    rows = jnp.concatenate([block[:half], block[half:]], axis=1)
+    lane = lax.broadcasted_iota(jnp.int32, rows.shape, 1) % HALF_LANES
+    owner = upper_ref[count].astype(jnp.float32)[:half]
+    packed_ref[0] = jnp.where(lane < vectors, rows, owner).astype(jnp.bfloat16)
+
+
+def face_block(lower, upper):
+    return pl.pallas_call(
+        face_kernel,
+        out_shape=jax.ShapeDtypeStruct((1, lower.shape[1] // 2, LANES), jnp.bfloat16),
+        in_specs=[pl.BlockSpec(memory_space=pltpu.VMEM)] * 2,
+        out_specs=pl.BlockSpec(memory_space=pltpu.VMEM),
+        compiler_params=pltpu.CompilerParams(vmem_limit_bytes=16 * 1024 * 1024),
+        name="face_block",
+    )(lower, upper)
 
 
 def owner_sums(block, owner_lane):
@@ -196,7 +228,7 @@
     hubs = math.isqrt(groups)
     first = groups - hubs
     faces = [block]
-    for shift in range(hubs, groups, hubs):
+    for shift in sorted(range(hubs, groups, hubs), key=lambda d: -min(d, groups - d)):
         faces.append(lax.ppermute(block, "grp", [(h - shift, h) for h in range(first, groups)]))
     faces = jnp.concatenate(faces, axis=0)
     step = hubs // 2
@@ -205,21 +237,42 @@
         faces = jnp.concatenate([faces, lax.ppermute(faces, "grp", pairs)], axis=0)
         step //= 2
     served = lax.axis_index("grp") - hubs * jnp.arange(groups // hubs)
+    served = jnp.where(lax.axis_index("grp") >= first, served, groups)
     mine = faces[None, :, 0, owner_lane] == served[:, None].astype(jnp.bfloat16)
     return jnp.sum(
         jnp.where(mine[:, :, None, None], faces[None].astype(jnp.float32), 0.0), axis=1
     )
 
 
+def finish_kernel(kept_ref, *refs):
+    received, (flat_ref, rows_ref) = refs[:-2], refs[-2:]
+    rows = kept_ref[...]
+    for ref in received:
+        rows = rows + ref[...]
+    rows_ref[...] = rows
+    flatten_rows(rows_ref, flat_ref)
+
+
 def handed_back(sums):
     groups = lax.axis_size("grp")
     hubs = math.isqrt(groups)
     first = groups - hubs
-    owned = jnp.where(lax.axis_index("grp") >= first, sums[0], 0.0)
+    received = []
     for i in range(1, groups // hubs):
         pairs = [(h, h - hubs * i) for h in range(first, groups)]
-        owned = owned + lax.ppermute(sums[i], "grp", pairs)
-    return owned
+        received.append(lax.ppermute(sums[i], "grp", pairs))
+    half = sums[0].shape[0]
+    operands = [sums[0], *received]
+    return pl.pallas_call(
+        finish_kernel,
+        out_shape=jax.ShapeDtypeStruct((1, 4 * half * half), jnp.float32),
+        in_specs=[pl.BlockSpec(memory_space=pltpu.VMEM)] * len(operands),
+        out_specs=pl.BlockSpec(memory_space=pltpu.VMEM),
+        scratch_shapes=[pltpu.VMEM((half, LANES), jnp.float32)],
+        compiler_params=pltpu.CompilerParams(vmem_limit_bytes=16 * 1024 * 1024),
+        cost_estimate=pl.CostEstimate(flops=10**11, bytes_accessed=0, transcendentals=0),
+        name="finish",
+    )(*operands)
 
 
 def per_device(
@@ -237,7 +290,7 @@
     vectors, interface = basis_rows.shape
     partners = send_tiles.shape[2]
     groups = lax.axis_size("grp")
-    payload, outgoing = schur_tiles(
+    payload, outgoing, own = schur_tiles(
         basis_rows,
         bdiag.reshape(1, interface),
         interior[0],
@@ -246,26 +299,16 @@
         send_counts.reshape(1, partners),
         land_tiles.reshape(1, partners),
         face_tiles[0, 0],
+        owner_map,
     )
     arrived = lax.all_to_all(payload, "sub", split_axis=0, concat_axis=0, tiled=True)
 
-    incoming = lax.ppermute(outgoing, "grp", [(g, g + 1) for g in range(groups - 1)])
-    own = jnp.stack(
-        [
-            lax.dynamic_slice(basis_rows, (0, face_tiles[0, 0, 0, j] * LANES), (vectors, LANES))
-            for j in range(face_tiles.shape[3])
-        ]
-    )
-    face = jnp.einsum("jki,jli->kl", incoming, own, preferred_element_type=jnp.float32)
-    half = vectors // 2
-    owner = jnp.full((half, HALF_LANES - vectors), owner_map[0], jnp.int32).astype(jnp.bfloat16)
-    small = face.astype(jnp.bfloat16)
-    small = jnp.concatenate([small[:half], owner, small[half:], owner], axis=1)[None]
+    above = lax.ppermute(own, "grp", [(g, g - 1) for g in range(1, groups)])
+    small = face_block(outgoing, above)
     sums = owner_sums(small, vectors)
-    packed, sums = coupling_blocks(arrived, basis_rows, sums)
+    packed, coupling_in = coupling_blocks(arrived, basis_rows)
     returned = lax.all_to_all(packed, "sub", split_axis=0, concat_axis=0, tiled=True)
-    owned = unpack(handed_back(sums), vectors)[None, None]
-    coupling_in = flattened(packed)
+    owned = handed_back(sums)[None]
     coupling_out = flattened(returned)
     return (coupling_in[None, None], coupling_out[None, None], owned)
 

time: 90.3 us -> 88.8 us (0.983)
  the two profiles are of different devices: /device:TPU:1 before, /device:TPU:897 now
where the time goes in v4:
time: 88.8 us; the launch traced here: 88.3 us
  starting transfers between devices  39.1 us (44%)
  waiting for transfers between devices  33.3 us (37%)
  Pallas kernels  12.8 us (14%)
  between operations  1.57 us (2%)
  local copies, waits for them, and re-layouts  1.16 us (1%)
    all_to_all x1, starting transfers between devices, per_device(): lax.all_to_all(packed, 'sub', split_axis=0, concat_axis=0, tiled=True)  14.3 us
    all_to_all x1, waiting for transfers between devices, per_device(): lax.all_to_all(packed, 'sub', split_axis=0, concat_axis=0, tiled=True)  14.3 us
    all_to_all x1, starting transfers between devices, per_device(): lax.all_to_all(payload, 'sub', split_axis=0, concat_axis=0, tiled=True)  10.8 us
    ppermute x3, waiting for transfers between devices, owner_sums(): lax.ppermute(block, 'grp', [(h - shift, h) for h in range(first, groups)])  9.22 us
    pallas_call x1, Pallas kernels, schur_tiles(): pl.pallas_call(schur_kernel, out_shape=(jax.ShapeDtypeStruct((partners, v...  7.98 us
    ppermute x2, waiting for transfers between devices, owner_sums(): faces = jnp.concatenate([faces, lax.ppermute(faces, 'grp', pairs)], axis=0)  6.48 us
    ppermute x2, starting transfers between devices, owner_sums(): faces = jnp.concatenate([faces, lax.ppermute(faces, 'grp', pairs)], axis=0)  4.05 us
    ppermute x3, starting transfers between devices, owner_sums(): lax.ppermute(block, 'grp', [(h - shift, h) for h in range(first, groups)])  3.9 us
  transfers between devices with their start and end apart: 11, of which 5 were waited for; matrix products, arithmetic and copies ran while one was open for 1% of the time, Pallas kernels for 4%

profile of v4, /device:TPU:897, one launch (start us, length us, event | category | flops | bytes accessed | tf_op | source)
XLA Modules:
  0.0 88.3 jit_solution(7982909537592964278)
XLA Ops:
  0.6 0.0 copy-start
  1.4 8.0 %schur_tiles.1 = (bf16[64,56,128]{2,1,0:T(8,128)(2,1)}, bf16[4,48,128]{2,1,0:T(8,128)(2,1)}, bf16[5,48,128]{2,1,0:T(8,128)(2,1)}) custom-call(bf16[48,8192]{1,0:T(8,128)(2,1)} %bitcast.19, f32[1,8192]{1,0:T(1,128)} %bitcast.23, bf16[8192,512]{1,0:T(8,128)(2,1)} %bitcast.21, bf16[64,128]{1,0:T(8,128)(2,1)} %bitcast.24, s32[1,64]{1,0:T(1,128)} %bitcast.26, ...), custom_call_target="tpu_custom_call" | custom-call | tf_op jit(solution)/shard_map/schur_tiles/pallas_call | solution.py:87
  9.3 10.8 %all-to-all-start = ((bf16[64,56,128]{2,1,0:T(8,128)(2,1)}), bf16[64,56,128]{2,1,0:T(8,128)(2,1)S(1)}, u32[]{:S(2)}, u32[]{:S(2)}) async-start(bf16[64,56,128]{2,1,0:T(8,128)(2,1)} %get-tuple-element.8), calls=%async_computation | async-start | bytes 1835008 | tf_op jit(solution)/shard_map/all_to_all | solution.py:304
  20.2 2.2 %collective-permute-start = (bf16[5,48,128]{2,1,0:T(8,128)(2,1)}, bf16[5,48,128]{2,1,0:T(8,128)(2,1)S(1)}, u32[]{:S(2)}, u32[]{:S(2)}) collective-permute-start(bf16[5,48,128]{2,1,0:T(8,128)(2,1)} %get-tuple-element.12), channel_id=1, source_target_pairs={{64,0},{128,64},{192,128},{256,192},{320,256},{384,320},{448,384},... | collective-permute-start | bytes 184328 | tf_op jit(solution)/shard_map/ppermute | solution.py:306
  22.4 3.3 %collective-permute-done.upper_ref = bf16[5,48,128]{2,1,0:T(8,128)(2,1)S(1)} collective-permute-done((bf16[5,48,128]{2,1,0:T(8,128)(2,1)}, bf16[5,48,128]{2,1,0:T(8,128)(2,1)S(1)}, u32[]{:S(2)}, u32[]{:S(2)}) %collective-permute-start) | collective-permute-done | bytes 61472 | tf_op jit(solution)/shard_map/ppermute | solution.py:306
  25.6 0.8 copy-done.1
  26.4 0.2 face_block.1
  26.6 1.3 %collective-permute-start.1 = (bf16[1,24,128]{2,1,0:T(8,128)(2,1)S(1)}, bf16[1,24,128]{2,1,0:T(8,128)(2,1)S(1)}, u32[]{:S(2)}, u32[]{:S(2)}) collective-permute-start(bf16[1,24,128]{2,1,0:T(8,128)(2,1)S(1)} %face_block.1), channel_id=1, source_target_pairs={{256,768},{320,832},{384,896},{448,960},{257,769},{321,833},{385,8... | collective-permute-start | bytes 18440 | tf_op jit(solution)/shard_map/ppermute | solution.py:232
  28.0 1.3 %collective-permute-start.2 = (bf16[1,24,128]{2,1,0:T(8,128)(2,1)S(1)}, bf16[1,24,128]{2,1,0:T(8,128)(2,1)S(1)}, u32[]{:S(2)}, u32[]{:S(2)}) collective-permute-start(bf16[1,24,128]{2,1,0:T(8,128)(2,1)S(1)} %face_block.1), channel_id=1, source_target_pairs={{512,768},{576,832},{640,896},{704,960},{513,769},{577,833},{641,8... | collective-permute-start | bytes 18440 | tf_op jit(solution)/shard_map/ppermute | solution.py:232
  29.3 1.3 %collective-permute-start.3 = (bf16[1,24,128]{2,1,0:T(8,128)(2,1)S(1)}, bf16[1,24,128]{2,1,0:T(8,128)(2,1)S(1)}, u32[]{:S(2)}, u32[]{:S(2)}) collective-permute-start(bf16[1,24,128]{2,1,0:T(8,128)(2,1)S(1)} %face_block.1), channel_id=1, source_target_pairs={{0,768},{64,832},{128,896},{192,960},{1,769},{65,833},{129,897},{1... | collective-permute-start | bytes 18440 | tf_op jit(solution)/shard_map/ppermute | solution.py:232
  30.6 9.2 %collective-permute-done.1 = bf16[1,24,128]{2,1,0:T(8,128)(2,1)S(1)} collective-permute-done((bf16[1,24,128]{2,1,0:T(8,128)(2,1)S(1)}, bf16[1,24,128]{2,1,0:T(8,128)(2,1)S(1)}, u32[]{:S(2)}, u32[]{:S(2)}) %collective-permute-start.1) | collective-permute-done | bytes 6176 | tf_op jit(solution)/shard_map/ppermute | solution.py:232
  39.8 0.0 collective-permute-done.2
  39.8 0.0 collective-permute-done.3
  39.8 2.1 %collective-permute-start.4 = (bf16[4,24,128]{2,1,0:T(8,128)(2,1)S(1)}, bf16[4,24,128]{2,1,0:T(8,128)(2,1)S(1)}, u32[]{:S(2)}, u32[]{:S(2)}) collective-permute-start(bf16[4,24,128]{2,1,0:T(8,128)(2,1)S(1)} %pad_maximum_fusion), channel_id=1, source_target_pairs={{768,896},{832,960},{896,768},{960,832},{769,897},{833,961},{897,7... | collective-permute-start | bytes 73736 | tf_op jit(solution)/shard_map/ppermute | solution.py:237
  42.0 3.6 %collective-permute-done.4 = bf16[4,24,128]{2,1,0:T(8,128)(2,1)S(1)} collective-permute-done((bf16[4,24,128]{2,1,0:T(8,128)(2,1)S(1)}, bf16[4,24,128]{2,1,0:T(8,128)(2,1)S(1)}, u32[]{:S(2)}, u32[]{:S(2)}) %collective-permute-start.4) | collective-permute-done | bytes 24608 | tf_op jit(solution)/shard_map/ppermute | solution.py:237
  45.6 1.9 %collective-permute-start.5 = (bf16[8,24,128]{2,1,0:T(8,128)(2,1)S(1)}, bf16[8,24,128]{2,1,0:T(8,128)(2,1)S(1)}, u32[]{:S(2)}, u32[]{:S(2)}) collective-permute-start(bf16[8,24,128]{2,1,0:T(8,128)(2,1)S(1)} %get-tuple-element.17), channel_id=1, source_target_pairs={{768,832},{832,768},{896,960},{960,896},{769,833},{833,769},{897,9... | collective-permute-start | bytes 147464 | tf_op jit(solution)/shard_map/ppermute | solution.py:237
  47.5 2.9 %collective-permute-done.5 = bf16[8,24,128]{2,1,0:T(8,128)(2,1)S(1)} collective-permute-done((bf16[8,24,128]{2,1,0:T(8,128)(2,1)S(1)}, bf16[8,24,128]{2,1,0:T(8,128)(2,1)S(1)}, u32[]{:S(2)}, u32[]{:S(2)}) %collective-permute-start.5) | collective-permute-done | bytes 49184 | tf_op jit(solution)/shard_map/ppermute | solution.py:237
  50.5 0.3 slice_reduce_fusion
  50.7 0.1 broadcast_compare_fusion
  50.8 0.1 select_reduce_fusion
  51.0 1.3 %collective-permute-start.6 = (f32[24,128]{1,0:T(8,128)S(1)}, f32[24,128]{1,0:T(8,128)S(1)}, u32[]{:S(2)}, u32[]{:S(2)}) collective-permute-start(f32[24,128]{1,0:T(8,128)S(1)} %get-tuple-element.15), channel_id=1, source_target_pairs={{768,512},{832,576},{896,640},{960,704},{769,513},{833,577},{897,6... | collective-permute-start | bytes 36872 | tf_op jit(solution)/shard_map/ppermute | solution.py:263
  52.3 1.3 %collective-permute-start.7 = (f32[24,128]{1,0:T(8,128)S(1)}, f32[24,128]{1,0:T(8,128)S(1)}, u32[]{:S(2)}, u32[]{:S(2)}) collective-permute-start(f32[24,128]{1,0:T(8,128)S(1)} %get-tuple-element.14), channel_id=1, source_target_pairs={{768,256},{832,320},{896,384},{960,448},{769,257},{833,321},{897,3... | collective-permute-start | bytes 36872 | tf_op jit(solution)/shard_map/ppermute | solution.py:263
  53.6 1.3 %collective-permute-start.8 = (f32[24,128]{1,0:T(8,128)S(1)}, f32[24,128]{1,0:T(8,128)S(1)}, u32[]{:S(2)}, u32[]{:S(2)}) collective-permute-start(f32[24,128]{1,0:T(8,128)S(1)} %get-tuple-element.13), channel_id=1, source_target_pairs={{768,0},{832,64},{896,128},{960,192},{769,1},{833,65},{897,129},{9... | collective-permute-start | bytes 36872 | tf_op jit(solution)/shard_map/ppermute | solution.py:263
  54.9 0.0 all-to-all-done.arrived_ref
  54.9 2.9 %coupling_blocks.1 = (bf16[64,24,128]{2,1,0:T(8,128)(2,1)}, bf16[64,2304]{1,0:T(8,128)(2,1)}) custom-call(bf16[64,56,128]{2,1,0:T(8,128)(2,1)S(1)} %all-to-all-done.arrived_ref, bf16[48,8192]{1,0:T(8,128)(2,1)S(1)} %bitcast.20), custom_call_target="tpu_custom_call" | custom-call | tf_op jit(solution)/shard_map/coupling_blocks/pallas_call | solution.py:141
  57.8 14.3 %all-to-all-start.1 = ((bf16[64,24,128]{2,1,0:T(8,128)(2,1)}), bf16[64,24,128]{2,1,0:T(8,128)(2,1)S(1)}, u32[]{:S(2)}, u32[]{:S(2)}) async-start(bf16[64,24,128]{2,1,0:T(8,128)(2,1)} %get-tuple-element.10), calls=%async_computation.1 | async-start | bytes 786432 | tf_op jit(solution)/shard_map/all_to_all | solution.py:310
  72.2 0.0 collective-permute-done.6.refs_0_
  72.2 0.0 collective-permute-done.7.refs_1_
  72.2 0.0 collective-permute-done.8.refs_2_
  72.2 0.7 finish.1
  72.9 14.3 %all-to-all-done.1.packed_ref = bf16[64,24,128]{2,1,0:T(8,128)(2,1)S(1)} async-done(((bf16[64,24,128]{2,1,0:T(8,128)(2,1)}), bf16[64,24,128]{2,1,0:T(8,128)(2,1)S(1)}, u32[]{:S(2)}, u32[]{:S(2)}) %all-to-all-start.1) | async-done | bytes 393248 | tf_op jit(solution)/shard_map/all_to_all | solution.py:310
  87.2 1.0 %flatten.1 = bf16[64,2304]{1,0:T(8,128)(2,1)} custom-call(bf16[64,24,128]{2,1,0:T(8,128)(2,1)S(1)} %all-to-all-done.1.packed_ref), custom_call_target="tpu_custom_call" | custom-call | tf_op jit(solution)/shard_map/flatten/pallas_call | solution.py:191
  (12 shorter events, 0.1 us)
Async XLA Ops:
  0.6 54.3 %copy-start = (bf16[1,1,48,8192]{3,2,1,0:T(8,128)(2,1)S(1)}, bf16[1,1,48,8192]{3,2,1,0:T(8,128)(2,1)}, u32[]{:S(2)}) copy-start(bf16[1,1,48,8192]{3,2,1,0:T(8,128)(2,1)} %param.9) | copy-start | bytes 2359300
  9.3 45.5 %all-to-all-start = ((bf16[64,56,128]{2,1,0:T(8,128)(2,1)}), bf16[64,56,128]{2,1,0:T(8,128)(2,1)S(1)}, u32[]{:S(2)}, u32[]{:S(2)}) async-start(bf16[64,56,128]{2,1,0:T(8,128)(2,1)} %get-tuple-element.8), calls=%async_computation | async-start | bytes 1835008 | tf_op jit(solution)/shard_map/all_to_all | solution.py:304
  20.2 5.5 %collective-permute-start = (bf16[5,48,128]{2,1,0:T(8,128)(2,1)}, bf16[5,48,128]{2,1,0:T(8,128)(2,1)S(1)}, u32[]{:S(2)}, u32[]{:S(2)}) collective-permute-start(bf16[5,48,128]{2,1,0:T(8,128)(2,1)} %get-tuple-element.12), channel_id=1, source_target_pairs={{64,0},{128,64},{192,128},{256,192},{320,256},{384,320},{448,384},... | collective-permute-start | bytes 184328 | tf_op jit(solution)/shard_map/ppermute | solution.py:306
  25.6 0.8 copy-start.1
  26.6 13.2 %collective-permute-start.1 = (bf16[1,24,128]{2,1,0:T(8,128)(2,1)S(1)}, bf16[1,24,128]{2,1,0:T(8,128)(2,1)S(1)}, u32[]{:S(2)}, u32[]{:S(2)}) collective-permute-start(bf16[1,24,128]{2,1,0:T(8,128)(2,1)S(1)} %face_block.1), channel_id=1, source_target_pairs={{256,768},{320,832},{384,896},{448,960},{257,769},{321,833},{385,8... | collective-permute-start | bytes 18440 | tf_op jit(solution)/shard_map/ppermute | solution.py:232
  28.0 11.8 %collective-permute-start.2 = (bf16[1,24,128]{2,1,0:T(8,128)(2,1)S(1)}, bf16[1,24,128]{2,1,0:T(8,128)(2,1)S(1)}, u32[]{:S(2)}, u32[]{:S(2)}) collective-permute-start(bf16[1,24,128]{2,1,0:T(8,128)(2,1)S(1)} %face_block.1), channel_id=1, source_target_pairs={{512,768},{576,832},{640,896},{704,960},{513,769},{577,833},{641,8... | collective-permute-start | bytes 18440 | tf_op jit(solution)/shard_map/ppermute | solution.py:232
  29.3 10.5 %collective-permute-start.3 = (bf16[1,24,128]{2,1,0:T(8,128)(2,1)S(1)}, bf16[1,24,128]{2,1,0:T(8,128)(2,1)S(1)}, u32[]{:S(2)}, u32[]{:S(2)}) collective-permute-start(bf16[1,24,128]{2,1,0:T(8,128)(2,1)S(1)} %face_block.1), channel_id=1, source_target_pairs={{0,768},{64,832},{128,896},{192,960},{1,769},{65,833},{129,897},{1... | collective-permute-start | bytes 18440 | tf_op jit(solution)/shard_map/ppermute | solution.py:232
  39.8 5.8 %collective-permute-start.4 = (bf16[4,24,128]{2,1,0:T(8,128)(2,1)S(1)}, bf16[4,24,128]{2,1,0:T(8,128)(2,1)S(1)}, u32[]{:S(2)}, u32[]{:S(2)}) collective-permute-start(bf16[4,24,128]{2,1,0:T(8,128)(2,1)S(1)} %pad_maximum_fusion), channel_id=1, source_target_pairs={{768,896},{832,960},{896,768},{960,832},{769,897},{833,961},{897,7... | collective-permute-start | bytes 73736 | tf_op jit(solution)/shard_map/ppermute | solution.py:237
  45.6 4.8 %collective-permute-start.5 = (bf16[8,24,128]{2,1,0:T(8,128)(2,1)S(1)}, bf16[8,24,128]{2,1,0:T(8,128)(2,1)S(1)}, u32[]{:S(2)}, u32[]{:S(2)}) collective-permute-start(bf16[8,24,128]{2,1,0:T(8,128)(2,1)S(1)} %get-tuple-element.17), channel_id=1, source_target_pairs={{768,832},{832,768},{896,960},{960,896},{769,833},{833,769},{897,9... | collective-permute-start | bytes 147464 | tf_op jit(solution)/shard_map/ppermute | solution.py:237
  51.0 21.2 %collective-permute-start.6 = (f32[24,128]{1,0:T(8,128)S(1)}, f32[24,128]{1,0:T(8,128)S(1)}, u32[]{:S(2)}, u32[]{:S(2)}) collective-permute-start(f32[24,128]{1,0:T(8,128)S(1)} %get-tuple-element.15), channel_id=1, source_target_pairs={{768,512},{832,576},{896,640},{960,704},{769,513},{833,577},{897,6... | collective-permute-start | bytes 36872 | tf_op jit(solution)/shard_map/ppermute | solution.py:263
  52.3 19.9 %collective-permute-start.7 = (f32[24,128]{1,0:T(8,128)S(1)}, f32[24,128]{1,0:T(8,128)S(1)}, u32[]{:S(2)}, u32[]{:S(2)}) collective-permute-start(f32[24,128]{1,0:T(8,128)S(1)} %get-tuple-element.14), channel_id=1, source_target_pairs={{768,256},{832,320},{896,384},{960,448},{769,257},{833,321},{897,3... | collective-permute-start | bytes 36872 | tf_op jit(solution)/shard_map/ppermute | solution.py:263
  53.6 18.6 %collective-permute-start.8 = (f32[24,128]{1,0:T(8,128)S(1)}, f32[24,128]{1,0:T(8,128)S(1)}, u32[]{:S(2)}, u32[]{:S(2)}) collective-permute-start(f32[24,128]{1,0:T(8,128)S(1)} %get-tuple-element.13), channel_id=1, source_target_pairs={{768,0},{832,64},{896,128},{960,192},{769,1},{833,65},{897,129},{9... | collective-permute-start | bytes 36872 | tf_op jit(solution)/shard_map/ppermute | solution.py:263
  57.8 29.4 %all-to-all-start.1 = ((bf16[64,24,128]{2,1,0:T(8,128)(2,1)}), bf16[64,24,128]{2,1,0:T(8,128)(2,1)S(1)}, u32[]{:S(2)}, u32[]{:S(2)}) async-start(bf16[64,24,128]{2,1,0:T(8,128)(2,1)} %get-tuple-element.10), calls=%async_computation.1 | async-start | bytes 786432 | tf_op jit(solution)/shard_map/all_to_all | solution.py:310

commit v5 on v4

--- a/solution.py
+++ b/solution.py
@@ -19,9 +19,9 @@
 
 def schur_kernel(
     basis_hbm, bdiag_hbm, interior_hbm, weight_hbm, send_hbm, count_hbm, land_hbm, face_hbm,
-    owner_ref, payload_ref, faces_ref, own_ref,
+    owner_hbm, payload_ref, faces_ref, own_ref,
     basis_ref, bdiag_ref, interior_ref, weight_ref, send_ref, count_ref, land_ref, face_ref,
-    tiles_ref, scaled_ref, sems, small_sems,
+    owner_ref, tiles_ref, scaled_ref, sems, small_sems,
 ):
     vectors, interface = basis_ref.shape
     partners = payload_ref.shape[0]
@@ -35,7 +35,7 @@
         chunk_copies[-1].start()
     small = [
         (bdiag_hbm, bdiag_ref), (weight_hbm, weight_ref), (send_hbm, send_ref),
-        (count_hbm, count_ref), (land_hbm, land_ref), (face_hbm, face_ref),
+        (count_hbm, count_ref), (land_hbm, land_ref), (face_hbm, face_ref), (owner_hbm, owner_ref),
     ]
     small_copies = [pltpu.make_async_copy(a, b, small_sems.at[i]) for i, (a, b) in enumerate(small)]
     for copy in small_copies:
@@ -83,7 +83,7 @@
 def schur_tiles(basis, bdiag, interior, weights, send, counts, land, face, owner):
     vectors, interface = basis.shape
     partners = weights.shape[0]
-    operands = (basis, bdiag, interior, weights, send, counts, land, face)
+    operands = (basis, bdiag, interior, weights, send, counts, land, face, owner)
     return pl.pallas_call(
         schur_kernel,
         out_shape=(
@@ -91,8 +91,7 @@
             jax.ShapeDtypeStruct((face.shape[1], vectors, LANES), jnp.bfloat16),
             jax.ShapeDtypeStruct((face.shape[1] + 1, vectors, LANES), jnp.bfloat16),
         ),
-        in_specs=[pl.BlockSpec(memory_space=pltpu.HBM)] * len(operands)
-        + [pl.BlockSpec(memory_space=pltpu.SMEM)],
+        in_specs=[pl.BlockSpec(memory_space=pltpu.HBM)] * len(operands),
         out_specs=[pl.BlockSpec(memory_space=pltpu.VMEM)] * 3,
         scratch_shapes=[
             pltpu.VMEM(basis.shape, basis.dtype),
@@ -103,14 +102,15 @@
             pltpu.SMEM(counts.shape, jnp.int32),
             pltpu.SMEM(land.shape, jnp.int32),
             pltpu.SMEM(face.shape, jnp.int32),
+            pltpu.SMEM(owner.shape, jnp.int32),
             pltpu.VMEM((interface // LANES, vectors, LANES), jnp.bfloat16),
             pltpu.VMEM(weights.shape, jnp.float32),
             pltpu.SemaphoreType.DMA((CHUNKS + 1,)),
-            pltpu.SemaphoreType.DMA((6,)),
+            pltpu.SemaphoreType.DMA((7,)),
         ],
         compiler_params=pltpu.CompilerParams(vmem_limit_bytes=60 * 1024 * 1024),
         name="schur_tiles",
-    )(*operands, owner)
+    )(*operands)
 
 
 def block_kernel(
@@ -219,11 +219,29 @@
         in_specs=[pl.BlockSpec(memory_space=pltpu.VMEM)] * 2,
         out_specs=pl.BlockSpec(memory_space=pltpu.VMEM),
         compiler_params=pltpu.CompilerParams(vmem_limit_bytes=16 * 1024 * 1024),
+        cost_estimate=pl.CostEstimate(flops=10**11, bytes_accessed=0, transcendentals=0),
         name="face_block",
     )(lower, upper)
 
 
-def owner_sums(block, owner_lane):
+def merge_kernel(near_ref, far_ref, after_ref, merged_ref):
+    count = near_ref.shape[0]
+    merged_ref[0:count] = near_ref[...]
+    merged_ref[count : 2 * count] = far_ref[...]
+
+
+def merged(near, far, after):
+    return pl.pallas_call(
+        merge_kernel,
+        out_shape=jax.ShapeDtypeStruct((2 * near.shape[0],) + near.shape[1:], near.dtype),
+        in_specs=[pl.BlockSpec(memory_space=pltpu.VMEM)] * 2 + [pl.BlockSpec(memory_space=pltpu.HBM)],
+        out_specs=pl.BlockSpec(memory_space=pltpu.VMEM),
+        compiler_params=pltpu.CompilerParams(vmem_limit_bytes=16 * 1024 * 1024),
+        name="merge",
+    )(near, far, after)
+
+
+def owner_sums(block, owner_lane, after):
     groups = lax.axis_size("grp")
     hubs = math.isqrt(groups)
     first = groups - hubs
@@ -234,7 +252,11 @@
     step = hubs // 2
     while step >= 1:
         pairs = [(first + h, first + (h ^ step)) for h in range(hubs)]
-        faces = jnp.concatenate([faces, lax.ppermute(faces, "grp", pairs)], axis=0)
+        others = lax.ppermute(faces, "grp", pairs)
+        if step > 1:
+            faces = jnp.concatenate([faces, others], axis=0)
+        else:
+            faces = merged(faces, others, after)
         step //= 2
     served = lax.axis_index("grp") - hubs * jnp.arange(groups // hubs)
     served = jnp.where(lax.axis_index("grp") >= first, served, groups)
@@ -305,8 +327,8 @@
 
     above = lax.ppermute(own, "grp", [(g, g - 1) for g in range(1, groups)])
     small = face_block(outgoing, above)
-    sums = owner_sums(small, vectors)
     packed, coupling_in = coupling_blocks(arrived, basis_rows)
+    sums = owner_sums(small, vectors, packed)
     returned = lax.all_to_all(packed, "sub", split_axis=0, concat_axis=0, tiled=True)
     owned = handed_back(sums)[None]
     coupling_out = flattened(returned)

time: 88.8 us -> 83.5 us (0.940)
  the two profiles are of different devices: /device:TPU:897 before, /device:TPU:1 now
where the time goes in v5:
time: 83.5 us; the launch traced here: 83 us
  starting transfers between devices  46.2 us (55%)
  waiting for transfers between devices  21 us (25%)
  Pallas kernels  12.9 us (15%)
  between operations  1.52 us (2%)
  local copies, waits for them, and re-layouts  1.13 us (1%)
    all_to_all x1, starting transfers between devices, per_device(): lax.all_to_all(payload, 'sub', split_axis=0, concat_axis=0, tiled=True)  18.2 us
    ppermute x3, starting transfers between devices, owner_sums(): lax.ppermute(block, 'grp', [(h - shift, h) for h in range(first, groups)])  16.3 us
    ppermute x3, waiting for transfers between devices, handed_back(): received.append(lax.ppermute(sums[i], 'grp', pairs))  8.09 us
    pallas_call x1, Pallas kernels, schur_tiles(): pl.pallas_call(schur_kernel, out_shape=(jax.ShapeDtypeStruct((partners, v...  7.99 us
    all_to_all x1, starting transfers between devices, per_device(): lax.all_to_all(packed, 'sub', split_axis=0, concat_axis=0, tiled=True)  6.47 us
    all_to_all x1, waiting for transfers between devices, per_device(): lax.all_to_all(packed, 'sub', split_axis=0, concat_axis=0, tiled=True)  6.24 us
    all_to_all x1, waiting for transfers between devices, per_device(): lax.all_to_all(payload, 'sub', split_axis=0, concat_axis=0, tiled=True)  5.91 us
    pallas_call x1, Pallas kernels, coupling_blocks(): pl.pallas_call(block_kernel, out_shape=(jax.ShapeDtypeStruct((partners, h...  2.9 us
  transfers between devices with their start and end apart: 11, of which 4 were waited for; matrix products, arithmetic and copies ran while one was open for 0% of the time, Pallas kernels for 5%

profile of v5, /device:TPU:1, one launch (start us, length us, event | category | flops | bytes accessed | tf_op | source)
XLA Modules:
  0.0 83.0 jit_solution(4389580176689604305)
XLA Ops:
  1.3 8.0 %schur_tiles.1 = (bf16[64,56,128]{2,1,0:T(8,128)(2,1)}, bf16[4,48,128]{2,1,0:T(8,128)(2,1)}, bf16[5,48,128]{2,1,0:T(8,128)(2,1)}) custom-call(bf16[48,8192]{1,0:T(8,128)(2,1)} %bitcast.19, f32[1,8192]{1,0:T(1,128)} %bitcast.23, bf16[8192,512]{1,0:T(8,128)(2,1)} %bitcast.21, bf16[64,128]{1,0:T(8,128)(2,1)} %bitcast.24, s32[1,64]{1,0:T(1,128)} %bitcast.26, ...), custom_call_target="tpu_custom_call" | custom-call | tf_op jit(solution)/shard_map/schur_tiles/pallas_call | solution.py:87
  9.3 1.3 %collective-permute-start = (bf16[5,48,128]{2,1,0:T(8,128)(2,1)}, bf16[5,48,128]{2,1,0:T(8,128)(2,1)S(1)}, u32[]{:S(2)}, u32[]{:S(2)}) collective-permute-start(bf16[5,48,128]{2,1,0:T(8,128)(2,1)} %get-tuple-element.12), channel_id=1, source_target_pairs={{64,0},{128,64},{192,128},{256,192},{320,256},{384,320},{448,384},... | collective-permute-start | bytes 184328 | tf_op jit(solution)/shard_map/ppermute | solution.py:328
  10.6 18.2 %all-to-all-start = ((bf16[64,56,128]{2,1,0:T(8,128)(2,1)}), bf16[64,56,128]{2,1,0:T(8,128)(2,1)S(1)}, u32[]{:S(2)}, u32[]{:S(2)}) async-start(bf16[64,56,128]{2,1,0:T(8,128)(2,1)} %get-tuple-element.8), calls=%async_computation | async-start | bytes 1835008 | tf_op jit(solution)/shard_map/all_to_all | solution.py:326
  28.8 0.0 collective-permute-done.upper_ref
  28.9 0.0 copy-start.1
  28.9 0.8 copy-done.1
  29.7 0.2 face_block.1
  29.9 0.8 collective-permute-start.1
  30.7 0.7 collective-permute-start.2
  31.4 14.8 %collective-permute-start.3 = (bf16[1,24,128]{2,1,0:T(8,128)(2,1)S(1)}, bf16[1,24,128]{2,1,0:T(8,128)(2,1)S(1)}, u32[]{:S(2)}, u32[]{:S(2)}) collective-permute-start(bf16[1,24,128]{2,1,0:T(8,128)(2,1)S(1)} %face_block.1), channel_id=1, source_target_pairs={{0,768},{64,832},{128,896},{192,960},{1,769},{65,833},{129,897},{1... | collective-permute-start | bytes 18440 | tf_op jit(solution)/shard_map/ppermute | solution.py:250
  46.2 0.0 collective-permute-done.1
  46.2 0.0 collective-permute-done.2
  46.2 0.7 collective-permute-done.3
  46.9 0.7 collective-permute-start.4
  47.6 0.0 collective-permute-done.4
  47.6 0.7 collective-permute-start.5
  48.3 5.9 %all-to-all-done.arrived_ref = bf16[64,56,128]{2,1,0:T(8,128)(2,1)S(1)} async-done(((bf16[64,56,128]{2,1,0:T(8,128)(2,1)}), bf16[64,56,128]{2,1,0:T(8,128)(2,1)S(1)}, u32[]{:S(2)}, u32[]{:S(2)}) %all-to-all-start) | async-done | bytes 917536 | tf_op jit(solution)/shard_map/all_to_all | solution.py:326
  54.3 2.9 %coupling_blocks.1 = (bf16[64,24,128]{2,1,0:T(8,128)(2,1)}, bf16[64,2304]{1,0:T(8,128)(2,1)}) custom-call(bf16[64,56,128]{2,1,0:T(8,128)(2,1)S(1)} %all-to-all-done.arrived_ref, bf16[48,8192]{1,0:T(8,128)(2,1)S(1)} %bitcast.20), custom_call_target="tpu_custom_call" | custom-call | tf_op jit(solution)/shard_map/coupling_blocks/pallas_call | solution.py:141
  57.2 0.0 collective-permute-done.5.far_ref
  57.2 0.3 slice_reduce_fusion
  57.5 0.1 broadcast_compare_fusion
  57.6 0.1 select_reduce_fusion
  57.8 0.7 collective-permute-start.6
  58.4 0.7 collective-permute-start.7
  59.1 1.3 %collective-permute-start.8 = (f32[24,128]{1,0:T(8,128)S(1)}, f32[24,128]{1,0:T(8,128)S(1)}, u32[]{:S(2)}, u32[]{:S(2)}) collective-permute-start(f32[24,128]{1,0:T(8,128)S(1)} %get-tuple-element.13), channel_id=1, source_target_pairs={{768,0},{832,64},{896,128},{960,192},{769,1},{833,65},{897,129},{9... | collective-permute-start | bytes 36872 | tf_op jit(solution)/shard_map/ppermute | solution.py:285
  60.4 6.5 %all-to-all-start.1 = ((bf16[64,24,128]{2,1,0:T(8,128)(2,1)}), bf16[64,24,128]{2,1,0:T(8,128)(2,1)S(1)}, u32[]{:S(2)}, u32[]{:S(2)}) async-start(bf16[64,24,128]{2,1,0:T(8,128)(2,1)} %get-tuple-element.10.after_ref), calls=%async_computation.1 | async-start | bytes 786432 | tf_op jit(solution)/shard_map/all_to_all | solution.py:332
  66.9 0.0 collective-permute-done.6.refs_0_
  66.9 0.0 collective-permute-done.7.refs_1_
  66.9 8.1 %collective-permute-done.8.refs_2_ = f32[24,128]{1,0:T(8,128)S(1)} collective-permute-done((f32[24,128]{1,0:T(8,128)S(1)}, f32[24,128]{1,0:T(8,128)S(1)}, u32[]{:S(2)}, u32[]{:S(2)}) %collective-permute-start.8) | collective-permute-done | bytes 12320 | tf_op jit(solution)/shard_map/ppermute | solution.py:285
  75.0 0.7 finish.1
  75.7 6.2 %all-to-all-done.1.packed_ref = bf16[64,24,128]{2,1,0:T(8,128)(2,1)S(1)} async-done(((bf16[64,24,128]{2,1,0:T(8,128)(2,1)}), bf16[64,24,128]{2,1,0:T(8,128)(2,1)S(1)}, u32[]{:S(2)}, u32[]{:S(2)}) %all-to-all-start.1) | async-done | bytes 393248 | tf_op jit(solution)/shard_map/all_to_all | solution.py:332
  81.9 1.0 %flatten.1 = bf16[64,2304]{1,0:T(8,128)(2,1)} custom-call(bf16[64,24,128]{2,1,0:T(8,128)(2,1)S(1)} %all-to-all-done.1.packed_ref), custom_call_target="tpu_custom_call" | custom-call | tf_op jit(solution)/shard_map/flatten/pallas_call | solution.py:191
  (12 shorter events, 0.1 us)
Async XLA Ops:
  9.3 19.6 %collective-permute-start = (bf16[5,48,128]{2,1,0:T(8,128)(2,1)}, bf16[5,48,128]{2,1,0:T(8,128)(2,1)S(1)}, u32[]{:S(2)}, u32[]{:S(2)}) collective-permute-start(bf16[5,48,128]{2,1,0:T(8,128)(2,1)} %get-tuple-element.12), channel_id=1, source_target_pairs={{64,0},{128,64},{192,128},{256,192},{320,256},{384,320},{448,384},... | collective-permute-start | bytes 184328 | tf_op jit(solution)/shard_map/ppermute | solution.py:328
  10.6 43.7 %all-to-all-start = ((bf16[64,56,128]{2,1,0:T(8,128)(2,1)}), bf16[64,56,128]{2,1,0:T(8,128)(2,1)S(1)}, u32[]{:S(2)}, u32[]{:S(2)}) async-start(bf16[64,56,128]{2,1,0:T(8,128)(2,1)} %get-tuple-element.8), calls=%async_computation | async-start | bytes 1835008 | tf_op jit(solution)/shard_map/all_to_all | solution.py:326
  28.9 0.8 copy-start.1
  29.7 24.6 %copy-start = (bf16[1,1,48,8192]{3,2,1,0:T(8,128)(2,1)S(1)}, bf16[1,1,48,8192]{3,2,1,0:T(8,128)(2,1)}, u32[]{:S(2)}) copy-start(bf16[1,1,48,8192]{3,2,1,0:T(8,128)(2,1)} %param.9) | copy-start | bytes 2359300
  29.9 16.3 %collective-permute-start.1 = (bf16[1,24,128]{2,1,0:T(8,128)(2,1)S(1)}, bf16[1,24,128]{2,1,0:T(8,128)(2,1)S(1)}, u32[]{:S(2)}, u32[]{:S(2)}) collective-permute-start(bf16[1,24,128]{2,1,0:T(8,128)(2,1)S(1)} %face_block.1), channel_id=1, source_target_pairs={{256,768},{320,832},{384,896},{448,960},{257,769},{321,833},{385,8... | collective-permute-start | bytes 18440 | tf_op jit(solution)/shard_map/ppermute | solution.py:250
  30.7 15.5 %collective-permute-start.2 = (bf16[1,24,128]{2,1,0:T(8,128)(2,1)S(1)}, bf16[1,24,128]{2,1,0:T(8,128)(2,1)S(1)}, u32[]{:S(2)}, u32[]{:S(2)}) collective-permute-start(bf16[1,24,128]{2,1,0:T(8,128)(2,1)S(1)} %face_block.1), channel_id=1, source_target_pairs={{512,768},{576,832},{640,896},{704,960},{513,769},{577,833},{641,8... | collective-permute-start | bytes 18440 | tf_op jit(solution)/shard_map/ppermute | solution.py:250
  31.4 15.6 %collective-permute-start.3 = (bf16[1,24,128]{2,1,0:T(8,128)(2,1)S(1)}, bf16[1,24,128]{2,1,0:T(8,128)(2,1)S(1)}, u32[]{:S(2)}, u32[]{:S(2)}) collective-permute-start(bf16[1,24,128]{2,1,0:T(8,128)(2,1)S(1)} %face_block.1), channel_id=1, source_target_pairs={{0,768},{64,832},{128,896},{192,960},{1,769},{65,833},{129,897},{1... | collective-permute-start | bytes 18440 | tf_op jit(solution)/shard_map/ppermute | solution.py:250
  46.9 0.7 collective-permute-start.4
  47.6 9.5 %collective-permute-start.5 = (bf16[8,24,128]{2,1,0:T(8,128)(2,1)S(1)}, bf16[8,24,128]{2,1,0:T(8,128)(2,1)S(1)}, u32[]{:S(2)}, u32[]{:S(2)}) collective-permute-start(bf16[8,24,128]{2,1,0:T(8,128)(2,1)S(1)} %constant_dynamic-update-slice_fusion.near_ref), channel_id=1, source_target_pairs={{768,832},{832,768},{896,960},{960,896},{769,833},{833,769},{897,9... | collective-permute-start | bytes 147464 | tf_op jit(solution)/shard_map/ppermute | solution.py:255
  57.8 9.1 %collective-permute-start.6 = (f32[24,128]{1,0:T(8,128)S(1)}, f32[24,128]{1,0:T(8,128)S(1)}, u32[]{:S(2)}, u32[]{:S(2)}) collective-permute-start(f32[24,128]{1,0:T(8,128)S(1)} %get-tuple-element.15), channel_id=1, source_target_pairs={{768,512},{832,576},{896,640},{960,704},{769,513},{833,577},{897,6... | collective-permute-start | bytes 36872 | tf_op jit(solution)/shard_map/ppermute | solution.py:285
  58.4 8.5 %collective-permute-start.7 = (f32[24,128]{1,0:T(8,128)S(1)}, f32[24,128]{1,0:T(8,128)S(1)}, u32[]{:S(2)}, u32[]{:S(2)}) collective-permute-start(f32[24,128]{1,0:T(8,128)S(1)} %get-tuple-element.14), channel_id=1, source_target_pairs={{768,256},{832,320},{896,384},{960,448},{769,257},{833,321},{897,3... | collective-permute-start | bytes 36872 | tf_op jit(solution)/shard_map/ppermute | solution.py:285
  59.1 15.9 %collective-permute-start.8 = (f32[24,128]{1,0:T(8,128)S(1)}, f32[24,128]{1,0:T(8,128)S(1)}, u32[]{:S(2)}, u32[]{:S(2)}) collective-permute-start(f32[24,128]{1,0:T(8,128)S(1)} %get-tuple-element.13), channel_id=1, source_target_pairs={{768,0},{832,64},{896,128},{960,192},{769,1},{833,65},{897,129},{9... | collective-permute-start | bytes 36872 | tf_op jit(solution)/shard_map/ppermute | solution.py:285
  60.4 21.5 %all-to-all-start.1 = ((bf16[64,24,128]{2,1,0:T(8,128)(2,1)}), bf16[64,24,128]{2,1,0:T(8,128)(2,1)S(1)}, u32[]{:S(2)}, u32[]{:S(2)}) async-start(bf16[64,24,128]{2,1,0:T(8,128)(2,1)} %get-tuple-element.10.after_ref), calls=%async_computation.1 | async-start | bytes 786432 | tf_op jit(solution)/shard_map/all_to_all | solution.py:332

commit v6 on v5

--- a/solution.py
+++ b/solution.py
@@ -21,7 +21,7 @@
     basis_hbm, bdiag_hbm, interior_hbm, weight_hbm, send_hbm, count_hbm, land_hbm, face_hbm,
     owner_hbm, payload_ref, faces_ref, own_ref,
     basis_ref, bdiag_ref, interior_ref, weight_ref, send_ref, count_ref, land_ref, face_ref,
-    owner_ref, tiles_ref, scaled_ref, sems, small_sems,
+    owner_ref, turned_ref, tiles_ref, scaled_ref, sems, small_sems,
 ):
     vectors, interface = basis_ref.shape
     partners = payload_ref.shape[0]
@@ -44,6 +44,8 @@
     total = jnp.zeros((vectors, interior_ref.shape[1]), jnp.float32)
     for i in range(CHUNKS):
         chunk_copies[i].wait()
+        rows = slice(i * chunk, (i + 1) * chunk)
+        turned_ref[:, rows] = jnp.transpose(interior_ref[rows, :])
         total += jnp.dot(
             basis_ref[:, i * chunk : (i + 1) * chunk],
             interior_ref[i * chunk : (i + 1) * chunk, :],
@@ -54,7 +56,7 @@
         copy.wait()
     for i in range(CHUNKS):
         cols = slice(i * chunk, (i + 1) * chunk)
-        correction = dot_nt(reduced, interior_ref[cols, :])
+        correction = jnp.dot(reduced, turned_ref[:, cols], preferred_element_type=jnp.float32)
         schur = (basis_ref[:, cols].astype(jnp.float32) * bdiag_ref[:, cols] - correction).astype(jnp.bfloat16)
         for j in range(chunk // LANES):
             tiles_ref[i * (chunk // LANES) + j] = schur[:, j * LANES : (j + 1) * LANES]
@@ -71,7 +73,7 @@
         ).astype(jnp.bfloat16)
         return carry
 
-    lax.fori_loop(0, partners, one, 0, unroll=4)
+    lax.fori_loop(0, partners, one, 0, unroll=16)
     for j in range(faces_ref.shape[0]):
         faces_ref[j] = tiles_ref[face_ref[1, j]]
         start = pl.multiple_of(face_ref[0, j] * LANES, LANES)
@@ -103,6 +105,7 @@
             pltpu.SMEM(land.shape, jnp.int32),
             pltpu.SMEM(face.shape, jnp.int32),
             pltpu.SMEM(owner.shape, jnp.int32),
+            pltpu.VMEM(interior.shape[::-1], interior.dtype),
             pltpu.VMEM((interface // LANES, vectors, LANES), jnp.bfloat16),
             pltpu.VMEM(weights.shape, jnp.float32),
             pltpu.SemaphoreType.DMA((CHUNKS + 1,)),

time: 83.5 us -> 82.8 us (level)
  no operation moved by 1% of the time
where the time goes in v6:
time: 82.8 us; the launch traced here: 82.3 us
  starting transfers between devices  46.2 us (56%)
  waiting for transfers between devices  21 us (25%)
  Pallas kernels  12.2 us (15%)
  between operations  1.52 us (2%)
  local copies, waits for them, and re-layouts  1.13 us (1%)
    all_to_all x1, starting transfers between devices, per_device(): lax.all_to_all(payload, 'sub', split_axis=0, concat_axis=0, tiled=True)  18.2 us
    ppermute x3, starting transfers between devices, owner_sums(): lax.ppermute(block, 'grp', [(h - shift, h) for h in range(first, groups)])  16.3 us
    ppermute x3, waiting for transfers between devices, handed_back(): received.append(lax.ppermute(sums[i], 'grp', pairs))  8.09 us
    pallas_call x1, Pallas kernels, schur_tiles(): pl.pallas_call(schur_kernel, out_shape=(jax.ShapeDtypeStruct((partners, v...  7.29 us
    all_to_all x1, starting transfers between devices, per_device(): lax.all_to_all(packed, 'sub', split_axis=0, concat_axis=0, tiled=True)  6.46 us
    all_to_all x1, waiting for transfers between devices, per_device(): lax.all_to_all(packed, 'sub', split_axis=0, concat_axis=0, tiled=True)  6.23 us
    all_to_all x1, waiting for transfers between devices, per_device(): lax.all_to_all(payload, 'sub', split_axis=0, concat_axis=0, tiled=True)  5.91 us
    pallas_call x1, Pallas kernels, coupling_blocks(): pl.pallas_call(block_kernel, out_shape=(jax.ShapeDtypeStruct((partners, h...  2.91 us
  transfers between devices with their start and end apart: 11, of which 4 were waited for; matrix products, arithmetic and copies ran while one was open for 0% of the time, Pallas kernels for 5%

profile of v6, /device:TPU:1, one launch (start us, length us, event | category | flops | bytes accessed | tf_op | source)
XLA Modules:
  0.0 82.3 jit_solution(2776804420816746960)
XLA Ops:
  1.3 7.3 %schur_tiles.1 = (bf16[64,56,128]{2,1,0:T(8,128)(2,1)}, bf16[4,48,128]{2,1,0:T(8,128)(2,1)}, bf16[5,48,128]{2,1,0:T(8,128)(2,1)}) custom-call(bf16[48,8192]{1,0:T(8,128)(2,1)} %bitcast.19, f32[1,8192]{1,0:T(1,128)} %bitcast.23, bf16[8192,512]{1,0:T(8,128)(2,1)} %bitcast.21, bf16[64,128]{1,0:T(8,128)(2,1)} %bitcast.24, s32[1,64]{1,0:T(1,128)} %bitcast.26, ...), custom_call_target="tpu_custom_call" | custom-call | tf_op jit(solution)/shard_map/schur_tiles/pallas_call | solution.py:89
  8.6 1.3 %collective-permute-start = (bf16[5,48,128]{2,1,0:T(8,128)(2,1)}, bf16[5,48,128]{2,1,0:T(8,128)(2,1)S(1)}, u32[]{:S(2)}, u32[]{:S(2)}) collective-permute-start(bf16[5,48,128]{2,1,0:T(8,128)(2,1)} %get-tuple-element.12), channel_id=1, source_target_pairs={{64,0},{128,64},{192,128},{256,192},{320,256},{384,320},{448,384},... | collective-permute-start | bytes 184328 | tf_op jit(solution)/shard_map/ppermute | solution.py:331
  9.9 18.2 %all-to-all-start = ((bf16[64,56,128]{2,1,0:T(8,128)(2,1)}), bf16[64,56,128]{2,1,0:T(8,128)(2,1)S(1)}, u32[]{:S(2)}, u32[]{:S(2)}) async-start(bf16[64,56,128]{2,1,0:T(8,128)(2,1)} %get-tuple-element.8), calls=%async_computation | async-start | bytes 1835008 | tf_op jit(solution)/shard_map/all_to_all | solution.py:329
  28.1 0.0 collective-permute-done.upper_ref
  28.2 0.0 copy-start.1
  28.2 0.8 copy-done.1
  29.0 0.2 face_block.1
  29.2 0.7 collective-permute-start.1
  29.9 0.7 collective-permute-start.2
  30.5 14.9 %collective-permute-start.3 = (bf16[1,24,128]{2,1,0:T(8,128)(2,1)S(1)}, bf16[1,24,128]{2,1,0:T(8,128)(2,1)S(1)}, u32[]{:S(2)}, u32[]{:S(2)}) collective-permute-start(bf16[1,24,128]{2,1,0:T(8,128)(2,1)S(1)} %face_block.1), channel_id=1, source_target_pairs={{0,768},{64,832},{128,896},{192,960},{1,769},{65,833},{129,897},{1... | collective-permute-start | bytes 18440 | tf_op jit(solution)/shard_map/ppermute | solution.py:253
  45.5 0.0 collective-permute-done.1
  45.5 0.0 collective-permute-done.2
  45.5 0.7 collective-permute-done.3
  46.2 0.7 collective-permute-start.4
  46.9 0.0 collective-permute-done.4
  46.9 0.7 collective-permute-start.5
  47.6 5.9 %all-to-all-done.arrived_ref = bf16[64,56,128]{2,1,0:T(8,128)(2,1)S(1)} async-done(((bf16[64,56,128]{2,1,0:T(8,128)(2,1)}), bf16[64,56,128]{2,1,0:T(8,128)(2,1)S(1)}, u32[]{:S(2)}, u32[]{:S(2)}) %all-to-all-start) | async-done | bytes 917536 | tf_op jit(solution)/shard_map/all_to_all | solution.py:329
  53.6 2.9 %coupling_blocks.1 = (bf16[64,24,128]{2,1,0:T(8,128)(2,1)}, bf16[64,2304]{1,0:T(8,128)(2,1)}) custom-call(bf16[64,56,128]{2,1,0:T(8,128)(2,1)S(1)} %all-to-all-done.arrived_ref, bf16[48,8192]{1,0:T(8,128)(2,1)S(1)} %bitcast.20), custom_call_target="tpu_custom_call" | custom-call | tf_op jit(solution)/shard_map/coupling_blocks/pallas_call | solution.py:144
  56.5 0.0 collective-permute-done.5.far_ref
  56.5 0.3 slice_reduce_fusion
  56.8 0.1 broadcast_compare_fusion
  56.9 0.1 select_reduce_fusion
  57.1 0.7 collective-permute-start.6
  57.7 0.7 collective-permute-start.7
  58.4 1.3 %collective-permute-start.8 = (f32[24,128]{1,0:T(8,128)S(1)}, f32[24,128]{1,0:T(8,128)S(1)}, u32[]{:S(2)}, u32[]{:S(2)}) collective-permute-start(f32[24,128]{1,0:T(8,128)S(1)} %get-tuple-element.13), channel_id=1, source_target_pairs={{768,0},{832,64},{896,128},{960,192},{769,1},{833,65},{897,129},{9... | collective-permute-start | bytes 36872 | tf_op jit(solution)/shard_map/ppermute | solution.py:288
  59.7 6.5 %all-to-all-start.1 = ((bf16[64,24,128]{2,1,0:T(8,128)(2,1)}), bf16[64,24,128]{2,1,0:T(8,128)(2,1)S(1)}, u32[]{:S(2)}, u32[]{:S(2)}) async-start(bf16[64,24,128]{2,1,0:T(8,128)(2,1)} %get-tuple-element.10.after_ref), calls=%async_computation.1 | async-start | bytes 786432 | tf_op jit(solution)/shard_map/all_to_all | solution.py:335
  66.2 0.0 collective-permute-done.6.refs_0_
  66.2 0.0 collective-permute-done.7.refs_1_
  66.2 8.1 %collective-permute-done.8.refs_2_ = f32[24,128]{1,0:T(8,128)S(1)} collective-permute-done((f32[24,128]{1,0:T(8,128)S(1)}, f32[24,128]{1,0:T(8,128)S(1)}, u32[]{:S(2)}, u32[]{:S(2)}) %collective-permute-start.8) | collective-permute-done | bytes 12320 | tf_op jit(solution)/shard_map/ppermute | solution.py:288
  74.3 0.7 finish.1
  75.0 6.2 %all-to-all-done.1.packed_ref = bf16[64,24,128]{2,1,0:T(8,128)(2,1)S(1)} async-done(((bf16[64,24,128]{2,1,0:T(8,128)(2,1)}), bf16[64,24,128]{2,1,0:T(8,128)(2,1)S(1)}, u32[]{:S(2)}, u32[]{:S(2)}) %all-to-all-start.1) | async-done | bytes 393248 | tf_op jit(solution)/shard_map/all_to_all | solution.py:335
  81.2 1.0 %flatten.1 = bf16[64,2304]{1,0:T(8,128)(2,1)} custom-call(bf16[64,24,128]{2,1,0:T(8,128)(2,1)S(1)} %all-to-all-done.1.packed_ref), custom_call_target="tpu_custom_call" | custom-call | tf_op jit(solution)/shard_map/flatten/pallas_call | solution.py:194
  (12 shorter events, 0.1 us)
Async XLA Ops:
  8.6 19.6 %collective-permute-start = (bf16[5,48,128]{2,1,0:T(8,128)(2,1)}, bf16[5,48,128]{2,1,0:T(8,128)(2,1)S(1)}, u32[]{:S(2)}, u32[]{:S(2)}) collective-permute-start(bf16[5,48,128]{2,1,0:T(8,128)(2,1)} %get-tuple-element.12), channel_id=1, source_target_pairs={{64,0},{128,64},{192,128},{256,192},{320,256},{384,320},{448,384},... | collective-permute-start | bytes 184328 | tf_op jit(solution)/shard_map/ppermute | solution.py:331
  9.9 43.7 %all-to-all-start = ((bf16[64,56,128]{2,1,0:T(8,128)(2,1)}), bf16[64,56,128]{2,1,0:T(8,128)(2,1)S(1)}, u32[]{:S(2)}, u32[]{:S(2)}) async-start(bf16[64,56,128]{2,1,0:T(8,128)(2,1)} %get-tuple-element.8), calls=%async_computation | async-start | bytes 1835008 | tf_op jit(solution)/shard_map/all_to_all | solution.py:329
  28.2 0.8 copy-start.1
  29.0 24.6 %copy-start = (bf16[1,1,48,8192]{3,2,1,0:T(8,128)(2,1)S(1)}, bf16[1,1,48,8192]{3,2,1,0:T(8,128)(2,1)}, u32[]{:S(2)}) copy-start(bf16[1,1,48,8192]{3,2,1,0:T(8,128)(2,1)} %param.9) | copy-start | bytes 2359300
  29.2 16.3 %collective-permute-start.1 = (bf16[1,24,128]{2,1,0:T(8,128)(2,1)S(1)}, bf16[1,24,128]{2,1,0:T(8,128)(2,1)S(1)}, u32[]{:S(2)}, u32[]{:S(2)}) collective-permute-start(bf16[1,24,128]{2,1,0:T(8,128)(2,1)S(1)} %face_block.1), channel_id=1, source_target_pairs={{256,768},{320,832},{384,896},{448,960},{257,769},{321,833},{385,8... | collective-permute-start | bytes 18440 | tf_op jit(solution)/shard_map/ppermute | solution.py:253
  29.9 15.6 %collective-permute-start.2 = (bf16[1,24,128]{2,1,0:T(8,128)(2,1)S(1)}, bf16[1,24,128]{2,1,0:T(8,128)(2,1)S(1)}, u32[]{:S(2)}, u32[]{:S(2)}) collective-permute-start(bf16[1,24,128]{2,1,0:T(8,128)(2,1)S(1)} %face_block.1), channel_id=1, source_target_pairs={{512,768},{576,832},{640,896},{704,960},{513,769},{577,833},{641,8... | collective-permute-start | bytes 18440 | tf_op jit(solution)/shard_map/ppermute | solution.py:253
  30.5 15.7 %collective-permute-start.3 = (bf16[1,24,128]{2,1,0:T(8,128)(2,1)S(1)}, bf16[1,24,128]{2,1,0:T(8,128)(2,1)S(1)}, u32[]{:S(2)}, u32[]{:S(2)}) collective-permute-start(bf16[1,24,128]{2,1,0:T(8,128)(2,1)S(1)} %face_block.1), channel_id=1, source_target_pairs={{0,768},{64,832},{128,896},{192,960},{1,769},{65,833},{129,897},{1... | collective-permute-start | bytes 18440 | tf_op jit(solution)/shard_map/ppermute | solution.py:253
  46.2 0.7 collective-permute-start.4
  46.9 9.5 %collective-permute-start.5 = (bf16[8,24,128]{2,1,0:T(8,128)(2,1)S(1)}, bf16[8,24,128]{2,1,0:T(8,128)(2,1)S(1)}, u32[]{:S(2)}, u32[]{:S(2)}) collective-permute-start(bf16[8,24,128]{2,1,0:T(8,128)(2,1)S(1)} %constant_dynamic-update-slice_fusion.near_ref), channel_id=1, source_target_pairs={{768,832},{832,768},{896,960},{960,896},{769,833},{833,769},{897,9... | collective-permute-start | bytes 147464 | tf_op jit(solution)/shard_map/ppermute | solution.py:258
  57.1 9.1 %collective-permute-start.6 = (f32[24,128]{1,0:T(8,128)S(1)}, f32[24,128]{1,0:T(8,128)S(1)}, u32[]{:S(2)}, u32[]{:S(2)}) collective-permute-start(f32[24,128]{1,0:T(8,128)S(1)} %get-tuple-element.15), channel_id=1, source_target_pairs={{768,512},{832,576},{896,640},{960,704},{769,513},{833,577},{897,6... | collective-permute-start | bytes 36872 | tf_op jit(solution)/shard_map/ppermute | solution.py:288
  57.7 8.4 %collective-permute-start.7 = (f32[24,128]{1,0:T(8,128)S(1)}, f32[24,128]{1,0:T(8,128)S(1)}, u32[]{:S(2)}, u32[]{:S(2)}) collective-permute-start(f32[24,128]{1,0:T(8,128)S(1)} %get-tuple-element.14), channel_id=1, source_target_pairs={{768,256},{832,320},{896,384},{960,448},{769,257},{833,321},{897,3... | collective-permute-start | bytes 36872 | tf_op jit(solution)/shard_map/ppermute | solution.py:288
  58.4 15.9 %collective-permute-start.8 = (f32[24,128]{1,0:T(8,128)S(1)}, f32[24,128]{1,0:T(8,128)S(1)}, u32[]{:S(2)}, u32[]{:S(2)}) collective-permute-start(f32[24,128]{1,0:T(8,128)S(1)} %get-tuple-element.13), channel_id=1, source_target_pairs={{768,0},{832,64},{896,128},{960,192},{769,1},{833,65},{897,129},{9... | collective-permute-start | bytes 36872 | tf_op jit(solution)/shard_map/ppermute | solution.py:288
  59.7 21.5 %all-to-all-start.1 = ((bf16[64,24,128]{2,1,0:T(8,128)(2,1)}), bf16[64,24,128]{2,1,0:T(8,128)(2,1)S(1)}, u32[]{:S(2)}, u32[]{:S(2)}) async-start(bf16[64,24,128]{2,1,0:T(8,128)(2,1)} %get-tuple-element.10.after_ref), calls=%async_computation.1 | async-start | bytes 786432 | tf_op jit(solution)/shard_map/all_to_all | solution.py:335

commit v7 on v6

--- a/solution.py
+++ b/solution.py
@@ -9,7 +9,7 @@
 
 LANES = 128
 INDEX_ROWS = 8
-CHUNKS = 8
+CHUNKS = 16
 HALF_LANES = 64
 
 

time: 82.8 us -> 83 us (level)
  no operation moved by 1% of the time
where the time goes in v7:
time: 83 us; the launch traced here: 82.5 us
  starting transfers between devices  46.2 us (56%)
  waiting for transfers between devices  21 us (25%)
  Pallas kernels  12.4 us (15%)
  between operations  1.52 us (2%)
  local copies, waits for them, and re-layouts  1.13 us (1%)
    all_to_all x1, starting transfers between devices, per_device(): lax.all_to_all(payload, 'sub', split_axis=0, concat_axis=0, tiled=True)  18.2 us
    ppermute x3, starting transfers between devices, owner_sums(): lax.ppermute(block, 'grp', [(h - shift, h) for h in range(first, groups)])  16.3 us
    ppermute x3, waiting for transfers between devices, handed_back(): received.append(lax.ppermute(sums[i], 'grp', pairs))  8.1 us
    pallas_call x1, Pallas kernels, schur_tiles(): pl.pallas_call(schur_kernel, out_shape=(jax.ShapeDtypeStruct((partners, v...  7.52 us
    all_to_all x1, starting transfers between devices, per_device(): lax.all_to_all(packed, 'sub', split_axis=0, concat_axis=0, tiled=True)  6.47 us
    all_to_all x1, waiting for transfers between devices, per_device(): lax.all_to_all(packed, 'sub', split_axis=0, concat_axis=0, tiled=True)  6.23 us
    all_to_all x1, waiting for transfers between devices, per_device(): lax.all_to_all(payload, 'sub', split_axis=0, concat_axis=0, tiled=True)  5.91 us
    pallas_call x1, Pallas kernels, coupling_blocks(): pl.pallas_call(block_kernel, out_shape=(jax.ShapeDtypeStruct((partners, h...  2.9 us
  transfers between devices with their start and end apart: 11, of which 4 were waited for; matrix products, arithmetic and copies ran while one was open for 0% of the time, Pallas kernels for 5%

profile of v7, /device:TPU:1, one launch (start us, length us, event | category | flops | bytes accessed | tf_op | source)
XLA Modules:
  0.0 82.5 jit_solution(3077189764052120896)
XLA Ops:
  1.3 7.5 %schur_tiles.1 = (bf16[64,56,128]{2,1,0:T(8,128)(2,1)}, bf16[4,48,128]{2,1,0:T(8,128)(2,1)}, bf16[5,48,128]{2,1,0:T(8,128)(2,1)}) custom-call(bf16[48,8192]{1,0:T(8,128)(2,1)} %bitcast.19, f32[1,8192]{1,0:T(1,128)} %bitcast.23, bf16[8192,512]{1,0:T(8,128)(2,1)} %bitcast.21, bf16[64,128]{1,0:T(8,128)(2,1)} %bitcast.24, s32[1,64]{1,0:T(1,128)} %bitcast.26, ...), custom_call_target="tpu_custom_call" | custom-call | tf_op jit(solution)/shard_map/schur_tiles/pallas_call | solution.py:89
  8.8 1.3 %collective-permute-start = (bf16[5,48,128]{2,1,0:T(8,128)(2,1)}, bf16[5,48,128]{2,1,0:T(8,128)(2,1)S(1)}, u32[]{:S(2)}, u32[]{:S(2)}) collective-permute-start(bf16[5,48,128]{2,1,0:T(8,128)(2,1)} %get-tuple-element.12), channel_id=1, source_target_pairs={{64,0},{128,64},{192,128},{256,192},{320,256},{384,320},{448,384},... | collective-permute-start | bytes 184328 | tf_op jit(solution)/shard_map/ppermute | solution.py:331
  10.1 18.2 %all-to-all-start = ((bf16[64,56,128]{2,1,0:T(8,128)(2,1)}), bf16[64,56,128]{2,1,0:T(8,128)(2,1)S(1)}, u32[]{:S(2)}, u32[]{:S(2)}) async-start(bf16[64,56,128]{2,1,0:T(8,128)(2,1)} %get-tuple-element.8), calls=%async_computation | async-start | bytes 1835008 | tf_op jit(solution)/shard_map/all_to_all | solution.py:329
  28.4 0.0 collective-permute-done.upper_ref
  28.4 0.0 copy-start.1
  28.4 0.8 copy-done.1
  29.2 0.2 face_block.1
  29.4 0.7 collective-permute-start.1
  30.1 0.7 collective-permute-start.2
  30.7 14.9 %collective-permute-start.3 = (bf16[1,24,128]{2,1,0:T(8,128)(2,1)S(1)}, bf16[1,24,128]{2,1,0:T(8,128)(2,1)S(1)}, u32[]{:S(2)}, u32[]{:S(2)}) collective-permute-start(bf16[1,24,128]{2,1,0:T(8,128)(2,1)S(1)} %face_block.1), channel_id=1, source_target_pairs={{0,768},{64,832},{128,896},{192,960},{1,769},{65,833},{129,897},{1... | collective-permute-start | bytes 18440 | tf_op jit(solution)/shard_map/ppermute | solution.py:253
  45.7 0.0 collective-permute-done.1
  45.7 0.0 collective-permute-done.2
  45.7 0.7 collective-permute-done.3
  46.5 0.7 collective-permute-start.4
  47.1 0.0 collective-permute-done.4
  47.2 0.7 collective-permute-start.5
  47.9 5.9 %all-to-all-done.arrived_ref = bf16[64,56,128]{2,1,0:T(8,128)(2,1)S(1)} async-done(((bf16[64,56,128]{2,1,0:T(8,128)(2,1)}), bf16[64,56,128]{2,1,0:T(8,128)(2,1)S(1)}, u32[]{:S(2)}, u32[]{:S(2)}) %all-to-all-start) | async-done | bytes 917536 | tf_op jit(solution)/shard_map/all_to_all | solution.py:329
  53.8 2.9 %coupling_blocks.1 = (bf16[64,24,128]{2,1,0:T(8,128)(2,1)}, bf16[64,2304]{1,0:T(8,128)(2,1)}) custom-call(bf16[64,56,128]{2,1,0:T(8,128)(2,1)S(1)} %all-to-all-done.arrived_ref, bf16[48,8192]{1,0:T(8,128)(2,1)S(1)} %bitcast.20), custom_call_target="tpu_custom_call" | custom-call | tf_op jit(solution)/shard_map/coupling_blocks/pallas_call | solution.py:144
  56.7 0.0 collective-permute-done.5.far_ref
  56.7 0.3 slice_reduce_fusion
  57.0 0.1 broadcast_compare_fusion
  57.1 0.1 select_reduce_fusion
  57.3 0.7 collective-permute-start.6
  57.9 0.7 collective-permute-start.7
  58.6 1.3 %collective-permute-start.8 = (f32[24,128]{1,0:T(8,128)S(1)}, f32[24,128]{1,0:T(8,128)S(1)}, u32[]{:S(2)}, u32[]{:S(2)}) collective-permute-start(f32[24,128]{1,0:T(8,128)S(1)} %get-tuple-element.13), channel_id=1, source_target_pairs={{768,0},{832,64},{896,128},{960,192},{769,1},{833,65},{897,129},{9... | collective-permute-start | bytes 36872 | tf_op jit(solution)/shard_map/ppermute | solution.py:288
  59.9 6.5 %all-to-all-start.1 = ((bf16[64,24,128]{2,1,0:T(8,128)(2,1)}), bf16[64,24,128]{2,1,0:T(8,128)(2,1)S(1)}, u32[]{:S(2)}, u32[]{:S(2)}) async-start(bf16[64,24,128]{2,1,0:T(8,128)(2,1)} %get-tuple-element.10.after_ref), calls=%async_computation.1 | async-start | bytes 786432 | tf_op jit(solution)/shard_map/all_to_all | solution.py:335
  66.4 0.0 collective-permute-done.6.refs_0_
  66.4 0.0 collective-permute-done.7.refs_1_
  66.4 8.1 %collective-permute-done.8.refs_2_ = f32[24,128]{1,0:T(8,128)S(1)} collective-permute-done((f32[24,128]{1,0:T(8,128)S(1)}, f32[24,128]{1,0:T(8,128)S(1)}, u32[]{:S(2)}, u32[]{:S(2)}) %collective-permute-start.8) | collective-permute-done | bytes 12320 | tf_op jit(solution)/shard_map/ppermute | solution.py:288
  74.5 0.7 finish.1
  75.2 6.2 %all-to-all-done.1.packed_ref = bf16[64,24,128]{2,1,0:T(8,128)(2,1)S(1)} async-done(((bf16[64,24,128]{2,1,0:T(8,128)(2,1)}), bf16[64,24,128]{2,1,0:T(8,128)(2,1)S(1)}, u32[]{:S(2)}, u32[]{:S(2)}) %all-to-all-start.1) | async-done | bytes 393248 | tf_op jit(solution)/shard_map/all_to_all | solution.py:335
  81.5 1.0 %flatten.1 = bf16[64,2304]{1,0:T(8,128)(2,1)} custom-call(bf16[64,24,128]{2,1,0:T(8,128)(2,1)S(1)} %all-to-all-done.1.packed_ref), custom_call_target="tpu_custom_call" | custom-call | tf_op jit(solution)/shard_map/flatten/pallas_call | solution.py:194
  (12 shorter events, 0.1 us)
Async XLA Ops:
  8.8 19.6 %collective-permute-start = (bf16[5,48,128]{2,1,0:T(8,128)(2,1)}, bf16[5,48,128]{2,1,0:T(8,128)(2,1)S(1)}, u32[]{:S(2)}, u32[]{:S(2)}) collective-permute-start(bf16[5,48,128]{2,1,0:T(8,128)(2,1)} %get-tuple-element.12), channel_id=1, source_target_pairs={{64,0},{128,64},{192,128},{256,192},{320,256},{384,320},{448,384},... | collective-permute-start | bytes 184328 | tf_op jit(solution)/shard_map/ppermute | solution.py:331
  10.1 43.7 %all-to-all-start = ((bf16[64,56,128]{2,1,0:T(8,128)(2,1)}), bf16[64,56,128]{2,1,0:T(8,128)(2,1)S(1)}, u32[]{:S(2)}, u32[]{:S(2)}) async-start(bf16[64,56,128]{2,1,0:T(8,128)(2,1)} %get-tuple-element.8), calls=%async_computation | async-start | bytes 1835008 | tf_op jit(solution)/shard_map/all_to_all | solution.py:329
  28.4 0.8 copy-start.1
  29.2 24.6 %copy-start = (bf16[1,1,48,8192]{3,2,1,0:T(8,128)(2,1)S(1)}, bf16[1,1,48,8192]{3,2,1,0:T(8,128)(2,1)}, u32[]{:S(2)}) copy-start(bf16[1,1,48,8192]{3,2,1,0:T(8,128)(2,1)} %param.9) | copy-start | bytes 2359300
  29.4 16.3 %collective-permute-start.1 = (bf16[1,24,128]{2,1,0:T(8,128)(2,1)S(1)}, bf16[1,24,128]{2,1,0:T(8,128)(2,1)S(1)}, u32[]{:S(2)}, u32[]{:S(2)}) collective-permute-start(bf16[1,24,128]{2,1,0:T(8,128)(2,1)S(1)} %face_block.1), channel_id=1, source_target_pairs={{256,768},{320,832},{384,896},{448,960},{257,769},{321,833},{385,8... | collective-permute-start | bytes 18440 | tf_op jit(solution)/shard_map/ppermute | solution.py:253
  30.1 15.6 %collective-permute-start.2 = (bf16[1,24,128]{2,1,0:T(8,128)(2,1)S(1)}, bf16[1,24,128]{2,1,0:T(8,128)(2,1)S(1)}, u32[]{:S(2)}, u32[]{:S(2)}) collective-permute-start(bf16[1,24,128]{2,1,0:T(8,128)(2,1)S(1)} %face_block.1), channel_id=1, source_target_pairs={{512,768},{576,832},{640,896},{704,960},{513,769},{577,833},{641,8... | collective-permute-start | bytes 18440 | tf_op jit(solution)/shard_map/ppermute | solution.py:253
  30.7 15.7 %collective-permute-start.3 = (bf16[1,24,128]{2,1,0:T(8,128)(2,1)S(1)}, bf16[1,24,128]{2,1,0:T(8,128)(2,1)S(1)}, u32[]{:S(2)}, u32[]{:S(2)}) collective-permute-start(bf16[1,24,128]{2,1,0:T(8,128)(2,1)S(1)} %face_block.1), channel_id=1, source_target_pairs={{0,768},{64,832},{128,896},{192,960},{1,769},{65,833},{129,897},{1... | collective-permute-start | bytes 18440 | tf_op jit(solution)/shard_map/ppermute | solution.py:253
  46.5 0.7 collective-permute-start.4
  47.2 9.5 %collective-permute-start.5 = (bf16[8,24,128]{2,1,0:T(8,128)(2,1)S(1)}, bf16[8,24,128]{2,1,0:T(8,128)(2,1)S(1)}, u32[]{:S(2)}, u32[]{:S(2)}) collective-permute-start(bf16[8,24,128]{2,1,0:T(8,128)(2,1)S(1)} %constant_dynamic-update-slice_fusion.near_ref), channel_id=1, source_target_pairs={{768,832},{832,768},{896,960},{960,896},{769,833},{833,769},{897,9... | collective-permute-start | bytes 147464 | tf_op jit(solution)/shard_map/ppermute | solution.py:258
  57.3 9.1 %collective-permute-start.6 = (f32[24,128]{1,0:T(8,128)S(1)}, f32[24,128]{1,0:T(8,128)S(1)}, u32[]{:S(2)}, u32[]{:S(2)}) collective-permute-start(f32[24,128]{1,0:T(8,128)S(1)} %get-tuple-element.15), channel_id=1, source_target_pairs={{768,512},{832,576},{896,640},{960,704},{769,513},{833,577},{897,6... | collective-permute-start | bytes 36872 | tf_op jit(solution)/shard_map/ppermute | solution.py:288
  57.9 8.5 %collective-permute-start.7 = (f32[24,128]{1,0:T(8,128)S(1)}, f32[24,128]{1,0:T(8,128)S(1)}, u32[]{:S(2)}, u32[]{:S(2)}) collective-permute-start(f32[24,128]{1,0:T(8,128)S(1)} %get-tuple-element.14), channel_id=1, source_target_pairs={{768,256},{832,320},{896,384},{960,448},{769,257},{833,321},{897,3... | collective-permute-start | bytes 36872 | tf_op jit(solution)/shard_map/ppermute | solution.py:288
  58.6 15.9 %collective-permute-start.8 = (f32[24,128]{1,0:T(8,128)S(1)}, f32[24,128]{1,0:T(8,128)S(1)}, u32[]{:S(2)}, u32[]{:S(2)}) collective-permute-start(f32[24,128]{1,0:T(8,128)S(1)} %get-tuple-element.13), channel_id=1, source_target_pairs={{768,0},{832,64},{896,128},{960,192},{769,1},{833,65},{897,129},{9... | collective-permute-start | bytes 36872 | tf_op jit(solution)/shard_map/ppermute | solution.py:288
  59.9 21.5 %all-to-all-start.1 = ((bf16[64,24,128]{2,1,0:T(8,128)(2,1)}), bf16[64,24,128]{2,1,0:T(8,128)(2,1)S(1)}, u32[]{:S(2)}, u32[]{:S(2)}) async-start(bf16[64,24,128]{2,1,0:T(8,128)(2,1)} %get-tuple-element.10.after_ref), calls=%async_computation.1 | async-start | bytes 786432 | tf_op jit(solution)/shard_map/all_to_all | solution.py:335
